TPU v7x, 32 devices: a whole 2x2x4 slice. The times are simulated.
32 devices in a mesh: dp: 4 (over z), fsdp: 8 (over y, x, core).
Axes of the slice: x: 2, y: 2, z: 4, core: 2. Of those that a mesh axis runs over, the one named last changes fastest.
Arguments:
- patches: bfloat16 [4, 32, 1024, 768], P(None, ('dp', 'fsdp')), may hold values from -6 to 6
- labels: int32 [4, 32], P(None, ('dp', 'fsdp')), may hold values from 0 to 999
- valid: int32 [4, 32], P(None, ('dp', 'fsdp')), may hold values from 0 to 1, as said below
- mat3: float32 [320, 2560], P('fsdp'), may hold values from -0.3125 to 0.3125
- tall3: float32 [3328, 320], P('fsdp'), may hold values from -0.15625 to 0.15625
- mat4: float32 [512, 5096], P('fsdp'), may hold values from -0.25 to 0.25
- tall4: float32 [3328, 512], P('fsdp'), may hold values from -0.15625 to 0.15625
- depth: float32 [9, 3328], P(None, 'fsdp'), may hold values from -2 to 2
- norms3: float32 [8, 320], P(None, 'fsdp')
- norms4: float32 [8, 512], P(None, 'fsdp')
- mom_mat3: float32 [320, 2560], P('fsdp'), may hold values from -2.3841858e-07 to 2.3841858e-07
- mom_tall3: float32 [3328, 320], P('fsdp'), may hold values from -2.3841858e-07 to 2.3841858e-07
- mom_mat4: float32 [512, 5096], P('fsdp'), may hold values from -2.3841858e-07 to 2.3841858e-07
- mom_tall4: float32 [3328, 512], P('fsdp'), may hold values from -2.3841858e-07 to 2.3841858e-07
- mom_depth: float32 [9, 3328], P(None, 'fsdp'), may hold values from -2.3841858e-07 to 2.3841858e-07
- mom_norms3: float32 [8, 320], P(None, 'fsdp'), may hold values from -2.3841858e-07 to 2.3841858e-07
- mom_norms4: float32 [8, 512], P(None, 'fsdp'), may hold values from -2.3841858e-07 to 2.3841858e-07
- sq_mat3: float32 [320, 2560], P('fsdp'), may hold values from 1.6041436e-16 to 6.416574e-16
- sq_tall3: float32 [3328, 320], P('fsdp'), may hold values from 1.6041436e-16 to 6.416574e-16
- sq_mat4: float32 [512, 5096], P('fsdp'), may hold values from 1.6041436e-16 to 6.416574e-16
- sq_tall4: float32 [3328, 512], P('fsdp'), may hold values from 1.6041436e-16 to 6.416574e-16
- sq_depth: float32 [9, 3328], P(None, 'fsdp'), may hold values from 1.6041436e-16 to 6.416574e-16
- sq_norms3: float32 [8, 320], P(None, 'fsdp'), may hold values from 1.6041436e-16 to 6.416574e-16
- sq_norms4: float32 [8, 512], P(None, 'fsdp'), may hold values from 1.6041436e-16 to 6.416574e-16
Outputs:
- new_mat3: float32 [320, 2560], P('fsdp')
- new_tall3: float32 [3328, 320], P('fsdp')
- new_mat4: float32 [512, 5096], P('fsdp')
- new_tall4: float32 [3328, 512], P('fsdp')
- new_depth: float32 [9, 3328], P(None, 'fsdp')
- new_norms3: float32 [8, 320], P(None, 'fsdp')
- new_norms4: float32 [8, 512], P(None, 'fsdp')
- first_mat3: float32 [320, 2560], P('fsdp')
- first_tall3: float32 [3328, 320], P('fsdp')
- first_mat4: float32 [512, 5096], P('fsdp')
- first_tall4: float32 [3328, 512], P('fsdp')
- first_depth: float32 [9, 3328], P(None, 'fsdp')
- first_norms3: float32 [8, 320], P(None, 'fsdp')
- first_norms4: float32 [8, 512], P(None, 'fsdp')
- second_mat3: float32 [320, 2560], P('fsdp')
- second_tall3: float32 [3328, 320], P('fsdp')
- second_mat4: float32 [512, 5096], P('fsdp')
- second_tall4: float32 [3328, 512], P('fsdp')
- second_depth: float32 [9, 3328], P(None, 'fsdp')
- second_norms3: float32 [8, 320], P(None, 'fsdp')
- second_norms4: float32 [8, 512], P(None, 'fsdp')
- loss_sum: float32 [], replicated
- image_count: float32 [], replicated
- grad_norm: float32 [], replicated
Inputs may be any that keep to these rules, and one draw needn't show every extreme that they name: `valid`: 1 where the slot holds an image; in every micro-batch the last image slot holds one.
All inputs are finite; a program needn't handle non-finite values.
Results may differ from a plain program's by a relative error of at most 0.0078.
Values may be sent and summed in bfloat16 or wider, within the bound.
No kernel may reach another device: no remote copies, remote signals or barrier semaphores. Data moves between devices by JAX's collectives and lax.ppermute only.
A program may use at most 512 MiB of HBM per device.

v0:
```python
import jax
import jax.numpy as jnp
from jax import lax
from jax.sharding import PartitionSpec as P

H3 = 5
H4 = 8
GRID_ROWS = 32
GRID_COLS = 32
STEP = 10


eps_norm = 1e-06
smoothing = 0.1
clip_level = 0.001


def to_narrow(value):
    return lax.optimization_barrier(value.astype(jnp.bfloat16)).astype(jnp.float32)


def narrow_value(value):

    def plain(inner):
        return to_narrow(inner)

    def plain_keep(inner):
        return (to_narrow(inner), None)

    def plain_pass(kept, grad):
        return (grad,)

    wrapped = jax.custom_vjp(plain)
    wrapped.defvjp(plain_keep, plain_pass)
    return wrapped(value)


def narrow_grad(value):

    def plain(inner):
        return inner

    def plain_keep(inner):
        return (inner, None)

    def plain_low(kept, grad):
        return (to_narrow(grad),)

    wrapped = jax.custom_vjp(plain)
    wrapped.defvjp(plain_keep, plain_low)
    return wrapped(value)


def matmul(left, right):
    return jnp.dot(left, right, preferred_element_type=jnp.float32)


def contract(form, left, right):
    return jnp.einsum(form, left, right, preferred_element_type=jnp.float32)


def rounded(value):
    return narrow_grad(narrow_value(value))


def layer_norm(inputs, gain, shift):
    average = jnp.mean(inputs, axis=-1, keepdims=True)
    centred = inputs - average
    spread = jnp.mean(centred * centred, axis=-1, keepdims=True)
    return centred * lax.rsqrt(spread + eps_norm) * gain + shift


def merge_quads(inputs, row_count, column_count):
    width = inputs.shape[-1]
    squares = inputs.reshape(row_count // 2, 2, column_count // 2, 2, width).transpose(
        0, 2, 1, 3, 4
    )
    return squares.reshape(row_count // 2 * (column_count // 2), 4 * width)


def depthwise(inputs, kernel, row_count, column_count):
    width = inputs.shape[-1]
    padded = jnp.pad(inputs.reshape(row_count, column_count, width), ((1, 1), (1, 1), (0, 0)))
    total = jnp.zeros((row_count, column_count, width), jnp.float32)
    for offset in range(9):
        total = (
            total
            + padded[offset // 3 : offset // 3 + row_count, offset % 3 : offset % 3 + column_count]
            * kernel[offset]
        )
    return total.reshape(row_count * column_count, width)


def block(inputs, row_count, column_count, mat, w_second, kernel, gains, reduce_w, head_count):
    width = inputs.shape[-1]
    tokens = inputs.shape[0]
    normed = narrow_value(layer_norm(inputs, gains[0], gains[1]))
    query = rounded(matmul(normed, mat[:, :width]))
    if reduce_w is None:
        source = normed
        later = gains[2:]
    else:
        reduced = narrow_grad(matmul(merge_quads(normed, row_count, column_count), reduce_w))
        source = narrow_value(layer_norm(reduced, gains[2], gains[3]))
        later = gains[4:]
    keys_out = rounded(matmul(source, mat[:, width : 2 * width]))
    values_out = rounded(matmul(source, mat[:, 2 * width : 3 * width]))
    key_count = source.shape[0]
    head_size = width // head_count
    query_heads = query.reshape(tokens, head_count, head_size)
    key_heads = keys_out.reshape(key_count, head_count, head_size)
    value_heads = values_out.reshape(key_count, head_count, head_size)
    scores = narrow_grad(contract("qhd,khd->hqk", query_heads, key_heads) * head_size ** (-0.5))
    scores = scores - jnp.max(scores, axis=-1, keepdims=True)
    exponent = jnp.exp(scores)
    weights_soft = narrow_value(exponent / jnp.sum(exponent, axis=-1, keepdims=True))
    mixed = rounded(contract("hqk,khd->qhd", weights_soft, value_heads).reshape(tokens, width))
    after = inputs + narrow_grad(matmul(mixed, mat[:, 3 * width : 4 * width]))
    hidden_count = w_second.shape[0]
    normed = narrow_value(layer_norm(after, later[0], later[1]))
    hidden = narrow_grad(matmul(normed, mat[:, 4 * width : 4 * width + hidden_count]))
    activated = narrow_value(jax.nn.gelu(depthwise(hidden, kernel, row_count, column_count)))
    return after + narrow_grad(matmul(activated, w_second))


def image_loss(weights, pixels, target):
    mat3, tall3, mat4, tall4, depth, norms3, norms4 = [narrow_value(weight) for weight in weights]
    width3 = mat3.shape[0]
    width4 = mat4.shape[0]
    features = pixels.shape[-1]
    hidden3 = mat3.shape[1] - 4 * width3
    hidden4 = tall4.shape[0] - 4 * width3
    embedded = layer_norm(narrow_grad(matmul(pixels, tall3[:features])), norms3[0], norms3[1])
    state = block(
        embedded,
        GRID_ROWS,
        GRID_COLS,
        mat3,
        tall3[features + 4 * width3 :],
        depth[:, :hidden3],
        norms3[2:],
        tall3[features : features + 4 * width3],
        H3,
    )
    merged = merge_quads(narrow_value(state), GRID_ROWS, GRID_COLS)
    state = layer_norm(narrow_grad(matmul(merged, tall4[: 4 * width3])), norms4[0], norms4[1])
    state = block(
        state,
        GRID_ROWS // 2,
        GRID_COLS // 2,
        mat4,
        tall4[4 * width3 :],
        depth[:, hidden3:],
        norms4[2:6],
        None,
        H4,
    )
    pooled = narrow_value(jnp.mean(layer_norm(state, norms4[6], norms4[7]), axis=0, keepdims=True))
    logits = narrow_grad(matmul(pooled, mat4[:, 4 * width4 + hidden4 :]))[0]
    shifted = logits - jnp.max(logits)
    log_probs = shifted - jnp.log(jnp.sum(jnp.exp(shifted)))
    classes = logits.shape[0]
    one_hot = (jnp.arange(classes, dtype=jnp.int32) == target).astype(jnp.float32)
    return -jnp.sum(((1.0 - smoothing) * one_hot + smoothing / classes) * log_probs)


def group_loss(weights, pixel_group, target_group, present_group):

    def advance(running, element):
        pixels, target, present = element
        return (
            running
            + present * jax.checkpoint(image_loss)(weights, pixels.astype(jnp.float32), target),
            None,
        )

    running, unused = lax.scan(
        advance, jnp.float32(0.0), (pixel_group, target_group, present_group)
    )
    return running


def adamw(master, moment, second, gradient, is_norm):
    step_rate = 0.5 if is_norm else 0.05
    decay_now = 0.0 if is_norm else 0.05
    first = 0.9 * moment + 0.1 * gradient
    second_new = 0.999 * second + 0.001 * gradient * gradient
    first_hat = first / (1.0 - 0.9**STEP)
    second_hat = second_new / (1.0 - 0.999**STEP)
    updated = master - step_rate * (first_hat / (jnp.sqrt(second_hat) + 1e-08) + decay_now * master)
    return (updated, first, second_new)


def body(
    patches,
    labels,
    valid,
    mat3,
    tall3,
    mat4,
    tall4,
    depth,
    norms3,
    norms4,
    mom_mat3,
    mom_tall3,
    mom_mat4,
    mom_tall4,
    mom_depth,
    mom_norms3,
    mom_norms4,
    sq_mat3,
    sq_tall3,
    sq_mat4,
    sq_tall4,
    sq_depth,
    sq_norms3,
    sq_norms4,
):
    masters = (mat3, tall3, mat4, tall4, depth, norms3, norms4)
    moments = (mom_mat3, mom_tall3, mom_mat4, mom_tall4, mom_depth, mom_norms3, mom_norms4)
    seconds = (sq_mat3, sq_tall3, sq_mat4, sq_tall4, sq_depth, sq_norms3, sq_norms4)
    image_count = lax.psum(jnp.sum(valid).astype(jnp.float32), ("dp", "fsdp"))
    narrow = [master.astype(jnp.bfloat16) for master in masters]
    summed = None
    loss_local = jnp.float32(0.0)
    for micro in range(patches.shape[0]):
        gathered = (
            lax.all_gather(narrow[0], "fsdp", axis=0, tiled=True),
            lax.all_gather(narrow[1], "fsdp", axis=0, tiled=True),
            lax.all_gather(narrow[2], "fsdp", axis=0, tiled=True),
            lax.all_gather(narrow[3], "fsdp", axis=0, tiled=True),
            lax.all_gather(narrow[4], "fsdp", axis=1, tiled=True),
            lax.all_gather(narrow[5], "fsdp", axis=1, tiled=True),
            lax.all_gather(narrow[6], "fsdp", axis=1, tiled=True),
        )
        full_weights = tuple((piece.astype(jnp.float32) for piece in gathered))
        pixel_group = patches[micro]
        target_group = labels[micro]
        present_group = valid[micro].astype(jnp.float32)
        loss_value, pullback = jax.vjp(
            lambda weights_now: group_loss(weights_now, pixel_group, target_group, present_group),
            full_weights,
        )
        gradients = pullback(jnp.float32(1.0) / image_count)[0]
        loss_local = loss_local + loss_value
        summed = (
            gradients
            if summed is None
            else tuple((old + new for old, new in zip(summed, gradients)))
        )
    summed = (
        lax.psum_scatter(summed[0], "fsdp", scatter_dimension=0, tiled=True),
        lax.psum_scatter(summed[1], "fsdp", scatter_dimension=0, tiled=True),
        lax.psum_scatter(summed[2], "fsdp", scatter_dimension=0, tiled=True),
        lax.psum_scatter(summed[3], "fsdp", scatter_dimension=0, tiled=True),
        lax.psum_scatter(summed[4], "fsdp", scatter_dimension=1, tiled=True),
        lax.psum_scatter(summed[5], "fsdp", scatter_dimension=1, tiled=True),
        lax.psum_scatter(summed[6], "fsdp", scatter_dimension=1, tiled=True),
    )
    group = lax.psum(
        (summed[0], summed[1], summed[2], summed[3], summed[4], summed[5], summed[6]), "dp"
    )
    square_local = jnp.float32(0.0)
    for shard in group:
        square_local = square_local + jnp.sum(shard * shard)
    grad_norm = jnp.sqrt(lax.psum(square_local, "fsdp"))
    loss_sum = lax.psum(loss_local, ("dp", "fsdp"))
    clip_factor = jnp.minimum(1.0, clip_level / (grad_norm + 1e-06))
    results = [
        adamw(
            masters[place], moments[place], seconds[place], clip_factor * group[place], place >= 5
        )
        for place in range(7)
    ]
    return (
        results[0][0],
        results[1][0],
        results[2][0],
        results[3][0],
        results[4][0],
        results[5][0],
        results[6][0],
        results[0][1],
        results[1][1],
        results[2][1],
        results[3][1],
        results[4][1],
        results[5][1],
        results[6][1],
        results[0][2],
        results[1][2],
        results[2][2],
        results[3][2],
        results[4][2],
        results[5][2],
        results[6][2],
        loss_sum,
        image_count,
        grad_norm,
    )


def solution(mesh):
    in_specs = (
        P(None, ("dp", "fsdp"), None, None),
        P(None, ("dp", "fsdp")),
        P(None, ("dp", "fsdp")),
        P("fsdp", None),
        P("fsdp", None),
        P("fsdp", None),
        P("fsdp", None),
        P(None, "fsdp"),
        P(None, "fsdp"),
        P(None, "fsdp"),
        P("fsdp", None),
        P("fsdp", None),
        P("fsdp", None),
        P("fsdp", None),
        P(None, "fsdp"),
        P(None, "fsdp"),
        P(None, "fsdp"),
        P("fsdp", None),
        P("fsdp", None),
        P("fsdp", None),
        P("fsdp", None),
        P(None, "fsdp"),
        P(None, "fsdp"),
        P(None, "fsdp"),
    )
    out_specs = (
        P("fsdp", None),
        P("fsdp", None),
        P("fsdp", None),
        P("fsdp", None),
        P(None, "fsdp"),
        P(None, "fsdp"),
        P(None, "fsdp"),
        P("fsdp", None),
        P("fsdp", None),
        P("fsdp", None),
        P("fsdp", None),
        P(None, "fsdp"),
        P(None, "fsdp"),
        P(None, "fsdp"),
        P("fsdp", None),
        P("fsdp", None),
        P("fsdp", None),
        P("fsdp", None),
        P(None, "fsdp"),
        P(None, "fsdp"),
        P(None, "fsdp"),
        P(),
        P(),
        P(),
    )
    return jax.shard_map(body, mesh=mesh, in_specs=in_specs, out_specs=out_specs, check_vma=False)
```

profile of v0, /device:TPU:0, one launch (start us, length us, event | category | flops | bytes accessed | tf_op | source)
XLA Modules:
  0.0 2151.4 jit_solution(9762431816452615416)
XLA Ops:
  13.0 10.7 all-gather
  24.7 8.9 all-gather.1
  34.2 7.9 all-gather.2
  50.0 21.5 %all-gather.10.cloned.1.call-done = bf16[3328,320]{1,0:T(8,128)(2,1)} async-done(((bf16[416,320]{1,0:T(8,128)(2,1)}), bf16[3328,320]{1,0:T(8,128)(2,1)}) %all-gather.10.cloned.1.call-update) | async-done | bytes 2129936 | tf_op jit(solution)/shard_map/all_gather | solution.py:230
  87.9 13.5 reshape.3486
  151.7 5.2 fusion.894
  163.3 5.0 fusion.895
  174.8 4.3 fusion.897
  206.3 4.2 fusion.581
  214.5 67.9 %fusion.72 = (f32[32,32,1280]{2,1,0:T(8,128)}, f32[32,32,1280]{2,1,0:T(8,128)}, f32[32,32,1280]{2,1,0:T(8,128)}, f32[32,32,1280]{2,1,0:T(8,128)}) fusion(f32[32,32,1280]{2,1,0:T(8,128)} %bitcast.1184, f32[1280]{0:T(1024)S(1)} %copy-done.694, f32[1280]{0:T(1024)S(1)} %copy-done.695, f32[1280]{0:T(1024)S(1)} %copy-done.696, f32[1280]{0:T(1024)S(1)} %copy-done.697, ...), kind=kLoop, calls=%fused_computation.218 | loop fusion | flops 89128960 | bytes 41989120 | tf_op jit(solution)/shard_map/jvp()/while/body/eval_jaxpr/add | solution.py:87
  293.5 4.2 fusion.47
  400.4 30.5 %fusion.244 = (f32[16,16,2048]{2,1,0:T(8,128)}, f32[16,16,2048]{2,1,0:T(8,128)}, f32[16,16,2048]{2,1,0:T(8,128)}, f32[16,16,2048]{2,1,0:T(8,128)}) fusion(f32[16,16,2048]{2,1,0:T(8,128)} %bitcast.1216, f32[2048]{0:T(1024)S(1)} %bitcast.1608, f32[2048]{0:T(1024)S(1)} %bitcast.1607, f32[2048]{0:T(1024)S(1)} %bitcast.1606, f32[2048]{0:T(1024)S(1)} %bitcast.1605, ...), kind=kLoop, calls=%fused_computation.552 | loop fusion | flops 35651584 | bytes 16850944 | tf_op jit(solution)/shard_map/jvp()/while/body/eval_jaxpr/add | solution.py:87
  470.2 5.6 bitcast_convert_fusion.3
  475.8 39.6 %all-reduce.313 = (f32[]{:T(128)}, f32[]{:T(128)}) all-reduce(f32[]{:T(128)S(6)} %convert_element_type.2316, f32[]{:T(128)S(6)} %add.3841), channel_id=1, replica_groups=mesh['dp'=4,'fsdp'=8] {'dp','fsdp'}, use_global_device_ids=true, to_apply=%region_1.0 | all-reduce | flops 2 | bytes 16 | tf_op jit(solution)/shard_map/psum | solution.py:223
  544.3 19.8 multiply_add_fusion
  564.3 6.5 fusion.134
  621.5 6.1 multiply_reduce_fusion.56
  627.6 5.1 broadcast_multiply_fusion.40
  632.8 4.8 pad_add_fusion.24
  710.1 20.1 multiply_add_fusion.1
  730.2 6.5 fusion.137
  793.9 6.5 multiply_reduce_fusion.65
  800.4 5.2 broadcast_multiply_fusion.49
  805.6 4.8 pad_add_fusion.25
  854.3 27.3 %multiply_reduce_fusion.8 = (f32[1280]{0:T(1024)}, f32[1280]{0:T(1024)}, f32[1280]{0:T(1024)}, f32[1280]{0:T(1024)}, f32[1280]{0:T(1024)}, /*index=5*/f32[1280]{...) fusion(f32[32,32,1280]{2,1,0:T(8,128)} %bitcast.1163, f32[1024,1280]{1,0:T(8,128)} %get-tuple-element.2002, ...), kind=kOutput, calls=%fused_computation.334 | convolution fusion | flops 879482880 | bytes 22650880 | tf_op jit(solution)/shard_map/transpose(jvp())/while/body/eval_jaxpr/checkpoint/dot_general | solution.py:55
  881.7 17.0 broadcast_multiply_fusion
  898.6 8.4 pad_add_fusion
  907.1 11.7 fusion.128
  928.7 13.1 multiply_reduce_fusion.17
  941.8 17.0 broadcast_multiply_fusion.9
  958.8 8.4 pad_add_fusion.1
  967.3 11.7 fusion.129
  987.8 5.0 convert_reduce_fusion
  1036.0 20.3 multiply_add_fusion.2
  1056.3 6.5 fusion.140
  1113.4 6.1 multiply_reduce_fusion.74
  1119.5 5.0 broadcast_multiply_fusion.58
  1124.5 4.8 pad_add_fusion.26
  1201.8 20.5 multiply_add_fusion.3
  1222.5 6.5 fusion.143
  1285.3 6.5 multiply_reduce_fusion.83
  1291.9 5.0 broadcast_multiply_fusion.67
  1296.9 4.8 pad_add_fusion.27
  1345.6 26.8 %multiply_reduce_fusion.26 = (f32[1280]{0:T(1024)}, f32[1280]{0:T(1024)}, f32[1280]{0:T(1024)}, f32[1280]{0:T(1024)}, f32[1280]{0:T(1024)}, /*index=5*/f32[1280]...) fusion(f32[32,32,1280]{2,1,0:T(8,128)} %bitcast.1171, f32[1024,1280]{1,0:T(8,128)} %get-tuple-element.1980, ...), kind=kOutput, calls=%fused_computation.352 | convolution fusion | flops 879482880 | bytes 22650880 | tf_op jit(solution)/shard_map/transpose(jvp())/while/body/eval_jaxpr/checkpoint/dot_general | solution.py:55
  1372.4 17.0 broadcast_multiply_fusion.18
  1389.4 8.4 pad_add_fusion.2
  1397.9 11.6 fusion.130
  1419.5 13.1 multiply_reduce_fusion.35
  1432.6 17.0 broadcast_multiply_fusion.27
  1449.6 8.4 pad_add_fusion.3
  1458.1 11.9 fusion.131
  1478.8 5.0 convert_reduce_fusion.2
  1622.1 5.7 copy.499
  1665.9 9.2 add_add_fusion.1
  1711.8 17.3 add_add_fusion
  1730.0 4.8 multiply_reduce_fusion.4
  1762.7 39.9 %reduce-scatter.18.cloned.1.call-done = f32[416,512]{1,0:T(8,128)} async-done(((f32[3328,512]{1,0:T(8,128)}), f32[416,512]{1,0:T(8,128)}) %reduce-scatter.18.cloned.1.call-update) | async-done | bytes 851984 | tf_op jit(solution)/shard_map/reduce_scatter | solution.py:256
  1802.6 85.5 %reduce-scatter.16.cloned.1.call-done = f32[64,5096]{1,0:T(8,128)} async-done(((f32[512,5096]{1,0:T(8,128)}), f32[64,5096]{1,0:T(8,128)}) %reduce-scatter.16.cloned.1.call-update) | async-done | bytes 1304592 | tf_op jit(solution)/shard_map/reduce_scatter | solution.py:255
  1891.4 23.2 %all-reduce.312 = f32[8,320]{1,0:T(8,128)S(1)} all-reduce(f32[8,320]{1,0:T(8,128)S(1)} %add_add_fusion.54), channel_id=7, replica_groups=mesh['dp'=4,'fsdp'=8] {'fsdp'}, use_global_device_ids=true, to_apply=%region_313.314.clone | all-reduce | flops 2560 | bytes 20480
  1914.6 11.0 reduce-scatter.24.cloned.1.call-done
  1926.4 41.5 %reduce-scatter.22.cloned.1.call-done = f32[416,9]{1,0:T(8,128)} async-done(((f32[3328,9]{1,0:T(8,128)}), f32[416,9]{1,0:T(8,128)}) %reduce-scatter.22.cloned.1.call-update) | async-done | bytes 14992
  1968.9 20.3 all-reduce.314
  1991.1 105.7 %all-reduce.318.cloned.1.call-done = (f32[40,2560]{1,0:T(8,128)}, f32[416,320]{0,1:T(8,128)}, f32[64,5096]{1,0:T(8,128)}, f32[416,512]{1,0:T(8,128)}) async-done(((f32[40,2560]{1,0:T(8,128)}, f32[416,320]{0,1:T(8,128)}, f32[64,5096]{1,0:T(8,128)}, f32[416,512]{1,0:T(8,128)}), (f32[40,2560]{1,0:T(8,128)}, f32[416,320]{0,1:T(8,128)}, f32[64,5096]{1,0:T(8,128)}, ...) | async-done | bytes 3098640 | tf_op jit(solution)/shard_map/psum | solution.py:261
  2109.4 14.3 psum.78
  (3083 shorter events, 1077.7 us)
Async XLA Ops:
  7.2 42.8 %all-gather.8.cloned.1.call-start = ((), (), s32[]{:S(2)}) async-start(), calls=%async_computation.6 | async-start | bytes 1843200 | tf_op jit(solution)/shard_map/all_gather | solution.py:229
  9.1 62.4 %all-gather.10.cloned.1.call-start = ((), (), s32[]{:S(2)}) async-start(), calls=%async_computation.7 | async-start | bytes 2875392 | tf_op jit(solution)/shard_map/all_gather | solution.py:230
  11.1 310.3 %all-gather.14.cloned.1.call-start = ((), (), s32[]{:S(2)}) async-start(), calls=%async_computation.9 | async-start | bytes 3833856 | tf_op jit(solution)/shard_map/all_gather | solution.py:232
  11.9 22.3 %copy-start.760 = (f32[8,64]{1,0:T(8,128)S(1)}, f32[8,64]{1,0:T(8,128)}, u32[]{:S(2)}) copy-start(f32[8,64]{1,0:T(8,128)} %param.33) | copy-start | bytes 6148
  11.9 30.3 %copy-start.852 = (s32[4,1]{0,1:T(1,128)S(1)}, s32[4,1]{0,1:T(1,128)}, u32[]{:S(2)}) copy-start(s32[4,1]{0,1:T(1,128)} %param.25) | copy-start | bytes 52
  11.9 31.0 %copy-start.853 = (s32[4,1]{0,1:T(1,128)S(1)}, s32[4,1]{0,1:T(1,128)}, u32[]{:S(2)}) copy-start(s32[4,1]{0,1:T(1,128)} %param.26) | copy-start | bytes 52
  12.0 318.6 %all-gather.12.cloned.1.call-start = ((), (), s32[]{:S(2)}) async-start(), calls=%async_computation.8 | async-start | bytes 5898240 | tf_op jit(solution)/shard_map/all_gather | solution.py:231
  13.0 1747.5 %reduce-scatter.20.cloned.1.call-start = ((), (), s32[]{:S(2)}) async-start(), calls=%async_computation.13 | async-start | bytes 5750784
  23.9 50.0 %copy-start.101 = (bf16[3328,9]{0,1:T(8,128)(2,1)}, bf16[3328,9]{0,1:T(8,128)(2,1)S(1)}, u32[]{:S(2)}) copy-start(bf16[3328,9]{0,1:T(8,128)(2,1)S(1)} %reshape.3547) | copy-start | bytes 179716
  42.2 34.4 %copy-start.378 = (bf16[512,8]{0,1:T(8,128)(2,1)}, bf16[512,8]{0,1:T(8,128)(2,1)S(1)}, u32[]{:S(2)}) copy-start(bf16[512,8]{0,1:T(8,128)(2,1)S(1)} %reshape.3551) | copy-start | bytes 24580
  74.0 55.2 %copy-start.26 = (f32[1024,320]{0,1:T(8,128)}, f32[1024,320]{0,1:T(8,128)S(1)}, u32[]{:S(2)}) copy-start(f32[1024,320]{0,1:T(8,128)S(1)} %get-tuple-element.2179) | copy-start | bytes 3932164
  86.6 22.6 %copy-start.166 = (bf16[1024,320]{0,1:T(8,128)(2,1)}, bf16[1024,320]{0,1:T(8,128)(2,1)S(1)}, u32[]{:S(2)}) copy-start(bf16[1024,320]{0,1:T(8,128)(2,1)S(1)} %get-tuple-element.2148) | copy-start | bytes 1966084
  516.8 22.3 %copy-start.708 = (f32[320]{0:T(512)}, f32[320]{0:T(512)S(1)}, u32[]{:S(2)}) copy-start(f32[320]{0:T(512)S(1)} %get-tuple-element.1829) | copy-start | bytes 3844
  596.9 43.4 %copy-start.184 = (f32[256,512]{1,0:T(8,128)}, f32[256,512]{1,0:T(8,128)S(1)}, u32[]{:S(2)}) copy-start(f32[256,512]{1,0:T(8,128)S(1)} %get-tuple-element.2255) | copy-start | bytes 1572868
  681.9 22.9 %copy-start.712 = (f32[320]{0:T(512)}, f32[320]{0:T(512)S(1)}, u32[]{:S(2)}) copy-start(f32[320]{0:T(512)S(1)} %get-tuple-element.1821) | copy-start | bytes 3844
  765.2 48.0 %copy-start.185 = (f32[256,512]{1,0:T(8,128)}, f32[256,512]{1,0:T(8,128)S(1)}, u32[]{:S(2)}) copy-start(f32[256,512]{1,0:T(8,128)S(1)} %get-tuple-element.2278) | copy-start | bytes 1572868
  792.0 25.2 %copy-start.704 = (f32[256]{0:T(256)}, f32[256]{0:T(256)S(1)}, u32[]{:S(2)}) copy-start(f32[256]{0:T(256)S(1)} %multiply_multiply_fusion.54) | copy-start | bytes 3076
  793.6 23.6 %copy-start.764 = (f32[256]{0:T(256)}, f32[256]{0:T(256)S(1)}, u32[]{:S(2)}) copy-start(f32[256]{0:T(256)S(1)} %negate_multiply_fusion.23) | copy-start | bytes 3076
  854.2 27.4 %copy-start.515 = (f32[1280]{0:T(1024)S(1)}, f32[1280]{0:T(1024)}, u32[]{:S(2)}) copy-start(f32[1280]{0:T(1024)} %copy-done.514) | copy-start | bytes 15364
  854.2 27.4 %copy-start.517 = (f32[1280]{0:T(1024)S(1)}, f32[1280]{0:T(1024)}, u32[]{:S(2)}) copy-start(f32[1280]{0:T(1024)} %copy-done.516) | copy-start | bytes 15364
  854.2 27.4 %copy-start.519 = (f32[1280]{0:T(1024)S(1)}, f32[1280]{0:T(1024)}, u32[]{:S(2)}) copy-start(f32[1280]{0:T(1024)} %copy-done.518) | copy-start | bytes 15364
  854.2 27.4 %copy-start.521 = (f32[1280]{0:T(1024)S(1)}, f32[1280]{0:T(1024)}, u32[]{:S(2)}) copy-start(f32[1280]{0:T(1024)} %copy-done.520) | copy-start | bytes 15364
  854.2 27.4 %copy-start.523 = (f32[1280]{0:T(1024)S(1)}, f32[1280]{0:T(1024)}, u32[]{:S(2)}) copy-start(f32[1280]{0:T(1024)} %copy-done.522) | copy-start | bytes 15364
  854.3 27.4 %copy-start.525 = (f32[1280]{0:T(1024)S(1)}, f32[1280]{0:T(1024)}, u32[]{:S(2)}) copy-start(f32[1280]{0:T(1024)} %copy-done.524) | copy-start | bytes 15364
  854.3 27.4 %copy-start.527 = (f32[1280]{0:T(1024)S(1)}, f32[1280]{0:T(1024)}, u32[]{:S(2)}) copy-start(f32[1280]{0:T(1024)} %copy-done.526) | copy-start | bytes 15364
  854.3 27.4 %copy-start.529 = (f32[1280]{0:T(1024)S(1)}, f32[1280]{0:T(1024)}, u32[]{:S(2)}) copy-start(f32[1280]{0:T(1024)} %copy-done.528) | copy-start | bytes 15364
  854.3 27.4 %copy-start.531 = (f32[1280]{0:T(1024)S(1)}, f32[1280]{0:T(1024)}, u32[]{:S(2)}) copy-start(f32[1280]{0:T(1024)} %copy-done.530) | copy-start | bytes 15364
  898.6 26.0 %slice-start.14 = ((s8[5242880]{0:T(1024)(128)(4,1)}), s8[4194304]{0:T(1024)(128)(4,1)S(1)}, s32[]{:S(2)}) async-start(s8[5242880]{0:T(1024)(128)(4,1)} %bitcast.1154), calls=%async_computation.31 | async-start | bytes 8388608
  958.8 26.2 %slice-start.20 = ((s8[5242880]{0:T(1024)(128)(4,1)}), s8[4194304]{0:T(1024)(128)(4,1)S(1)}, s32[]{:S(2)}) async-start(s8[5242880]{0:T(1024)(128)(4,1)} %bitcast.1160), calls=%async_computation.37 | async-start | bytes 8388608
  1008.2 22.5 %copy-start.706 = (f32[320]{0:T(512)}, f32[320]{0:T(512)S(1)}, u32[]{:S(2)}) copy-start(f32[320]{0:T(512)S(1)} %get-tuple-element.1813) | copy-start | bytes 3844
  1088.9 43.1 %copy-start.186 = (f32[256,512]{1,0:T(8,128)}, f32[256,512]{1,0:T(8,128)S(1)}, u32[]{:S(2)}) copy-start(f32[256,512]{1,0:T(8,128)S(1)} %get-tuple-element.2301) | copy-start | bytes 1572868
  1173.6 22.9 %copy-start.710 = (f32[320]{0:T(512)}, f32[320]{0:T(512)S(1)}, u32[]{:S(2)}) copy-start(f32[320]{0:T(512)S(1)} %get-tuple-element.1805) | copy-start | bytes 3844
  1201.7 20.6 copy-start.532
  1201.7 20.6 copy-start.534
  1201.8 20.6 copy-start.536
  1201.8 20.6 copy-start.538
  1201.8 20.6 copy-start.540
  1201.8 20.6 copy-start.542
  1257.3 47.1 %copy-start.183 = (f32[256,512]{1,0:T(8,128)}, f32[256,512]{1,0:T(8,128)S(1)}, u32[]{:S(2)}) copy-start(f32[256,512]{1,0:T(8,128)S(1)} %get-tuple-element.2324) | copy-start | bytes 1572868
  1283.5 25.0 %copy-start.702 = (f32[256]{0:T(256)}, f32[256]{0:T(256)S(1)}, u32[]{:S(2)}) copy-start(f32[256]{0:T(256)S(1)} %multiply_multiply_fusion.62) | copy-start | bytes 3076
  1285.1 23.5 %copy-start.762 = (f32[256]{0:T(256)}, f32[256]{0:T(256)S(1)}, u32[]{:S(2)}) copy-start(f32[256]{0:T(256)S(1)} %negate_multiply_fusion.31) | copy-start | bytes 3076
  1345.5 26.8 %copy-start.497 = (f32[1280]{0:T(1024)S(1)}, f32[1280]{0:T(1024)}, u32[]{:S(2)}) copy-start(f32[1280]{0:T(1024)} %copy-done.496) | copy-start | bytes 15364
  1345.5 26.8 %copy-start.499 = (f32[1280]{0:T(1024)S(1)}, f32[1280]{0:T(1024)}, u32[]{:S(2)}) copy-start(f32[1280]{0:T(1024)} %copy-done.498) | copy-start | bytes 15364
  1345.6 26.8 %copy-start.501 = (f32[1280]{0:T(1024)S(1)}, f32[1280]{0:T(1024)}, u32[]{:S(2)}) copy-start(f32[1280]{0:T(1024)} %copy-done.500) | copy-start | bytes 15364
  1345.6 26.8 %copy-start.503 = (f32[1280]{0:T(1024)S(1)}, f32[1280]{0:T(1024)}, u32[]{:S(2)}) copy-start(f32[1280]{0:T(1024)} %copy-done.502) | copy-start | bytes 15364
  1345.6 26.8 %copy-start.505 = (f32[1280]{0:T(1024)S(1)}, f32[1280]{0:T(1024)}, u32[]{:S(2)}) copy-start(f32[1280]{0:T(1024)} %copy-done.504) | copy-start | bytes 15364
  1345.6 26.8 %copy-start.507 = (f32[1280]{0:T(1024)S(1)}, f32[1280]{0:T(1024)}, u32[]{:S(2)}) copy-start(f32[1280]{0:T(1024)} %copy-done.506) | copy-start | bytes 15364
  1345.6 26.8 %copy-start.509 = (f32[1280]{0:T(1024)S(1)}, f32[1280]{0:T(1024)}, u32[]{:S(2)}) copy-start(f32[1280]{0:T(1024)} %copy-done.508) | copy-start | bytes 15364
  1345.6 26.8 %copy-start.511 = (f32[1280]{0:T(1024)S(1)}, f32[1280]{0:T(1024)}, u32[]{:S(2)}) copy-start(f32[1280]{0:T(1024)} %copy-done.510) | copy-start | bytes 15364
  1345.6 26.8 %copy-start.513 = (f32[1280]{0:T(1024)S(1)}, f32[1280]{0:T(1024)}, u32[]{:S(2)}) copy-start(f32[1280]{0:T(1024)} %copy-done.512) | copy-start | bytes 15364
  1389.4 26.0 %slice-start.10 = ((s8[5242880]{0:T(1024)(128)(4,1)}), s8[4194304]{0:T(1024)(128)(4,1)S(1)}, s32[]{:S(2)}) async-start(s8[5242880]{0:T(1024)(128)(4,1)} %bitcast.1150), calls=%async_computation.27 | async-start | bytes 8388608
  1449.6 26.4 %slice-start.18 = ((s8[5242880]{0:T(1024)(128)(4,1)}), s8[4194304]{0:T(1024)(128)(4,1)S(1)}, s32[]{:S(2)}) async-start(s8[5242880]{0:T(1024)(128)(4,1)} %bitcast.1158), calls=%async_computation.35 | async-start | bytes 8388608
  1489.2 26.8 %copy-start.418 = (bf16[5,256,64]{1,2,0:T(8,128)(2,1)}, bf16[5,256,64]{1,2,0:T(8,128)(2,1)S(1)}, u32[]{:S(2)}) copy-start(bf16[5,256,64]{1,2,0:T(8,128)(2,1)S(1)} %fusion.442) | copy-start | bytes 491524
  1490.1 25.7 %copy-start.303 = (bf16[5,64,256]{2,1,0:T(8,128)(2,1)}, bf16[5,64,256]{2,1,0:T(8,128)(2,1)S(1)}, u32[]{:S(2)}) copy-start(bf16[5,64,256]{2,1,0:T(8,128)(2,1)S(1)} %convolution_convert_fusion.78) | copy-start | bytes 491524
  1495.8 27.9 %copy-start.420 = (bf16[5,256,64]{1,2,0:T(8,128)(2,1)}, bf16[5,256,64]{1,2,0:T(8,128)(2,1)S(1)}, u32[]{:S(2)}) copy-start(bf16[5,256,64]{1,2,0:T(8,128)(2,1)S(1)} %fusion.441) | copy-start | bytes 491524
  1497.8 25.7 %copy-start.305 = (bf16[5,64,256]{2,1,0:T(8,128)(2,1)}, bf16[5,64,256]{2,1,0:T(8,128)(2,1)S(1)}, u32[]{:S(2)}) copy-start(bf16[5,64,256]{2,1,0:T(8,128)(2,1)S(1)} %convolution_convert_fusion.79) | copy-start | bytes 491524
  1627.9 134.9 %reduce-scatter.14.cloned.1.call-start = ((), (), s32[]{:S(2)}) async-start(), calls=%async_computation.10 | async-start | bytes 3686400 | tf_op jit(solution)/shard_map/reduce_scatter | solution.py:253
  1649.2 153.4 %reduce-scatter.18.cloned.1.call-start = ((), (), s32[]{:S(2)}) async-start(), calls=%async_computation.12 | async-start | bytes 7667712 | tf_op jit(solution)/shard_map/reduce_scatter | solution.py:256
  1675.2 212.9 %reduce-scatter.16.cloned.1.call-start = ((), (), s32[]{:S(2)}) async-start(), calls=%async_computation.11 | async-start | bytes 11796480 | tf_op jit(solution)/shard_map/reduce_scatter | solution.py:255
  1729.2 196.4 %reduce-scatter.24.cloned.1.call-start = ((), (), s32[]{:S(2)}) async-start(), calls=%async_computation.15 | async-start | bytes 294912
  1757.4 210.4 %reduce-scatter.22.cloned.1.call-start = ((), (), s32[]{:S(2)}) async-start(), calls=%async_computation.14 | async-start | bytes 1916928
  1760.4 127.9 %copy-start.267 = (f32[416,320]{1,0:T(8,128)S(1)}, f32[416,320]{1,0:T(8,128)}, u32[]{:S(2)}) copy-start(f32[416,320]{1,0:T(8,128)} %param.28) | copy-start | bytes 1597444
  1760.4 336.3 %all-reduce.318.cloned.1.call-start = ((), (), s32[]{:S(2)}) async-start(), calls=%async_computation.16 | async-start | bytes 6455296 | tf_op jit(solution)/shard_map/psum | solution.py:261
  2098.6 26.0 %copy-start.252 = (f32[416,320]{0,1:T(8,128)S(1)}, f32[416,320]{0,1:T(8,128)}, u32[]{:S(2)}) copy-start(f32[416,320]{0,1:T(8,128)} %get-tuple-element.1871) | copy-start | bytes 1597444
  (910 other events, 3820.9 us)
Sparse Core Ops, SparseCore 0:
  10.5 28.6 all-gather.7
  41.7 29.8 all-gather.9
  74.0 33.4 all-gather.13
  109.8 41.1 all-gather.11
  1628.0 56.6 reduce-scatter.19
  1687.9 46.8 reduce-scatter.13
  1738.3 64.2 reduce-scatter.17
  1806.5 81.5 reduce-scatter.15
  1892.0 33.5 reduce-scatter.23
  1928.8 39.0 reduce-scatter.21
  1971.3 125.4 all-reduce.317
where the time goes:
time: 2170 us; the launch traced here: 2150 us
  other arithmetic  721 us (33%)
  matrix products  580 us (27%)
  local copies, waits for them, and re-layouts  362 us (17%)
  waiting for transfers between devices  305 us (14%)
  blocking collectives  125 us (6%)
  between operations  56.3 us (3%)
    dot_general x248, matrix products, matmul(): return jnp.dot(left, right, preferred_element_type=jnp.float32)  483 us
    add x10, other arithmetic, depthwise(): total + padded[offset // 3:offset // 3 + row_count, offset % 3:offset % 3...  191 us
    unnamed x1943, local copies, waits for them, and re-layouts  107 us
    psum x1, waiting for transfers between devices, body(): lax.psum((summed[0], summed[1], summed[2], summed[3], summed[4], summed[5...  106 us
    convert_element_type x77, other arithmetic, narrow_value(): return wrapped(value)  98.6 us
    reshape x32, local copies, waits for them, and re-layouts, merge_quads(): inputs.reshape(row_count // 2, 2, column_count // 2, 2, width)  91 us
    reshape x32, local copies, waits for them, and re-layouts, merge_quads(): return squares.reshape(row_count // 2 * (column_count // 2), 4 * width)  88.3 us
    mul x8, other arithmetic, depthwise(): padded[offset // 3:offset // 3 + row_count, offset % 3:offset % 3 + colum...  88.3 us
  transfers between devices with their start and end apart: 11, of which 6 were waited for; matrix products, arithmetic and copies ran while one was open for 18% of the time, Pallas kernels for 0%

commit v1 on v0

v1 whole, which is shorter than its diff:
```python
import functools

import jax
import jax.numpy as jnp
from jax import lax
from jax.experimental import pallas as pl
from jax.experimental.pallas import tpu as pltpu
from jax.sharding import PartitionSpec as P

BF = jnp.bfloat16
F32 = jnp.float32
C3 = 320
C3P = 384
H3 = 5
F3 = 1280
C4 = 512
H4 = 8
F4 = 2048
CLASSES = 1000
PATCH = 768
STEP = 10
IMGS = 4
TOK3 = 1024
TOK4 = 256
LC = 256
EPS = 1e-06
SMOOTHING = 0.1
CLIP_LEVEL = 0.001
SCALE = 0.125
VMEM_BYTES = 63 * 2**20


def contract(a, b, ca, cb):
    return lax.dot_general(a, b, (((ca,), (cb,)), ((), ())), preferred_element_type=F32)


def nn(a, b):
    return contract(a, b, 1, 0)


def nt(a, b):
    return contract(a, b, 1, 1)


def tn(a, b):
    return contract(a, b, 0, 0)


def normalize(x):
    centred = x - jnp.mean(x, axis=-1, keepdims=True)
    rstd = lax.rsqrt(jnp.mean(centred * centred, axis=-1, keepdims=True) + EPS)
    return centred * rstd, rstd


def norm_grad(dy, xhat, rstd, gain):
    dx = dy * gain
    return rstd * (dx - jnp.mean(dx, axis=-1, keepdims=True) - xhat * jnp.mean(dx * xhat, axis=-1, keepdims=True))


def column_sum(x):
    return jnp.sum(x, axis=0, keepdims=True)


def half_of(x, half):
    lane = lax.broadcasted_iota(jnp.int32, x.shape, 1)
    keep = (lane < 64) if half == 0 else (lane >= 64)
    return jnp.where(keep, x, jnp.zeros_like(x))


def softmax_rows0(scores):
    top = jnp.max(scores, axis=0, keepdims=True)
    exponent = jnp.exp(scores - top)
    return exponent * (1.0 / jnp.sum(exponent, axis=0, keepdims=True))


def gelu_both(c):
    k0 = 0.7978845608028654
    k1 = 0.044715 * k0
    c2 = c * c
    t = jnp.tanh(c * (k1 * c2 + k0))
    half = 0.5 * t + 0.5
    slope = half + c * (half - half * half) * (6.0 * k1 * c2 + 2.0 * k0)
    return c * half, slope


def shift_down(v):
    lane = lax.broadcasted_iota(jnp.int32, v.shape, 1)
    return jnp.where(lane == 0, 0.0, pltpu.roll(v, 1, 1))


def shift_up(v):
    lane = lax.broadcasted_iota(jnp.int32, v.shape, 1)
    return jnp.where(lane == 7, 0.0, pltpu.roll(v, 7, 1))


def class3(py, xm):
    return py * 4 + (xm & 1) * 2 + (xm >> 1)


def store3(plain, moved, plane, value):
    py, px = plane // 2, plane % 2
    value = value.reshape(2, 16, 8, value.shape[-1])
    for qx in range(2):
        plain[plane * 2 + qx, 1:17] = value[qx]
    if px == 1:
        moved[py * 2, 1:17] = shift_down(value[1])
    else:
        moved[py * 2 + 1, 1:17] = shift_up(value[0])


def tap3(plain, moved, py, xm, dy, dx, lanes):
    row = (py + dy) % 2
    start = 1 + (py + dy) // 2
    at = xm + dx
    if at == -1:
        return moved[row * 2, start : start + 16, :, lanes]
    if at == 4:
        return moved[row * 2 + 1, start : start + 16, :, lanes]
    return plain[class3(row, at), start : start + 16, :, lanes]


def store4(plain, moved, image, value):
    value = value.reshape(2, 16, 8, value.shape[-1])
    for qx in range(2):
        plain[image, qx, 1:17] = value[qx]
    moved[image, 0, 1:17] = shift_down(value[1])
    moved[image, 1, 1:17] = shift_up(value[0])


def tap4(plain, moved, image, qx, dy, dx, lanes):
    start = 1 + dy
    at = qx + dx
    if at == -1:
        return moved[image, 0, start : start + 16, :, lanes]
    if at == 2:
        return moved[image, 1, start : start + 16, :, lanes]
    return plain[image, at, start : start + 16, :, lanes]


TAPS = [(t, t // 3 - 1, t % 3 - 1) for t in range(9)]


def embed_attend(patches, tall3, mat3, norms, z_o, h_o, red_o, q_o, k_o, v_o, p_o, mix_o, x1_o, x0_s, vt_s):
    we = tall3[0:PATCH]
    reduced = None
    for b in range(4):
        rows = pl.ds(b * 256, 256)
        z = nn(patches[0, rows, :], we)
        z_o[0, rows, :] = z
        x0 = normalize(z)[0] * norms[0:1] + norms[1:2]
        x0_s[rows, :] = x0
        h = (normalize(x0)[0] * norms[2:3] + norms[3:4]).astype(BF)
        h_o[0, rows, :] = h
        q_o[0, rows, :] = nn(h, mat3[:, 0:C3P]).astype(BF)
        part = nn(h, tall3[PATCH + C3 * b : PATCH + C3 * (b + 1)])
        reduced = part if reduced is None else reduced + part
    red_o[0] = reduced
    r = (normalize(reduced)[0] * norms[4:5] + norms[5:6]).astype(BF)
    k = nn(r, mat3[:, C3P : 2 * C3P]).astype(BF)
    v = nn(r, mat3[:, 2 * C3P : 3 * C3P]).astype(BF)
    k_o[0] = k
    v_o[0] = v
    vt_s[...] = v.T

    def queries(b, carry):
        rows = pl.ds(pl.multiple_of(b * 256, 256), 256)
        for head in range(H3):
            lanes = slice(head // 2 * 128, head // 2 * 128 + 128)
            key = half_of(k_o[0, :, lanes], head % 2)
            scores = nt(key, q_o[0, rows, lanes]) * SCALE
            soft = softmax_rows0(scores).astype(BF)
            p_o[0, head, :, rows] = soft
            mix_o[0, head * 64 : head * 64 + 64, rows] = nn(vt_s[head * 64 : head * 64 + 64, :], soft).astype(BF)
        x1_o[0, rows, :] = x0_s[rows, :] + tn(mix_o[0, :, rows], mat3[0:C3, 3 * C3P : 3 * C3P + C3])
        return carry

    lax.fori_loop(0, 4, queries, 0)


def feed3(x1, tall3, mat3, depth, norms, n_o, hid_o, slope_o, act_o, x2_o, plain, moved):
    @pl.when(pl.program_id(0) == 0)
    def _():
        for ref in (plain, moved):
            ref[:, 0:1] = jnp.zeros((ref.shape[0], 1, 8, LC), F32)
            ref[:, 17:18] = jnp.zeros((ref.shape[0], 1, 8, LC), F32)

    for b in range(4):
        rows = pl.ds(b * 256, 256)
        n_o[0, rows, :] = (normalize(x1[0, rows, :])[0] * norms[6:7] + norms[7:8]).astype(BF)

    def chunk(j, carry):
        wide = pl.ds(pl.multiple_of(j * LC, LC), LC)
        w1 = mat3[:, pl.ds(pl.multiple_of(4 * C3P + j * LC, LC), LC)]
        for plane in range(4):
            rows = pl.ds(plane * 256, 256)
            value = nn(n_o[0, rows, :], w1)
            hid_o[0, rows, wide] = value.astype(BF)
            store3(plain, moved, plane, value)
        for lt in range(LC // 128):
            lanes = pl.ds(lt * 128, 128)
            out_lanes = pl.ds(pl.multiple_of(j * LC + lt * 128, 128), 128)
            kernel = depth[:, out_lanes]
            for py in range(2):
                for xm in range(4):
                    total = None
                    for t, dy, dx in TAPS:
                        term = tap3(plain, moved, py, xm, dy, dx, lanes) * kernel[t : t + 1][None]
                        total = term if total is None else total + term
                    act, slope = gelu_both(total)
                    rows = pl.ds(class3(py, xm) * 128, 128)
                    act_o[0, rows, out_lanes] = act.reshape(128, 128).astype(BF)
                    slope_o[0, rows, out_lanes] = slope.reshape(128, 128).astype(BF)
        return carry

    lax.fori_loop(0, F3 // LC, chunk, 0)
    for b in range(4):
        rows = pl.ds(b * 256, 256)
        x2_o[0, rows, :] = (x1[0, rows, :] + nn(act_o[0, rows, :], tall3[PATCH + 4 * C3 :])).astype(BF)


def section4(
    labels, valid, inv_count, x2, mat4, tall4, depth, norms,
    dx2_o, gm_o, gt_o, gd_o, gn_o, loss_o,
    first, y1_s, y2_s, h_s, qkv_s, p_s, mix_s, n_s, hid_s, slope_s, act_s, plain, moved, gd_s,
):
    for ref in (plain, moved):
        for at in (0, 17):
            ref[:, :, at : at + 1] = jnp.zeros((IMGS, 2, 1, 8, LC), F32)

    w1_at = 4 * C4
    wc_at = 4 * C4 + F4

    for i in range(IMGS):
        rows = pl.ds(i * TOK4, TOK4)
        prod = None
        for plane in range(4):
            part = nn(x2[i, plane * 256 : plane * 256 + 256, :], tall4[plane * C3 : plane * C3 + C3, :])
            prod = part if prod is None else prod + part
        first[rows, :] = prod
        y0 = normalize(prod)[0] * norms[0:1] + norms[1:2]
        y1_s[rows, :] = y0
        h_s[rows, :] = (normalize(y0)[0] * norms[2:3] + norms[3:4]).astype(BF)
    for j in range(3):
        wide = slice(j * C4, j * C4 + C4)
        qkv_s[:, wide] = nn(h_s[...], mat4[:, wide]).astype(BF)

    def attend(i, carry):
        rows = pl.ds(pl.multiple_of(i * TOK4, TOK4), TOK4)
        for head in range(H4):
            pair = head // 2 * 128
            key = half_of(qkv_s[rows, C4 + pair : C4 + pair + 128], head % 2)
            scores = nt(key, qkv_s[rows, pair : pair + 128]) * SCALE
            soft = softmax_rows0(scores).astype(BF)
            p_s[i * H4 + head] = soft
            if head % 2 == 0:
                vt = qkv_s[rows, 2 * C4 + pair : 2 * C4 + pair + 128].T
            half = vt[0:64] if head % 2 == 0 else vt[64:128]
            mix_s[head * 64 : head * 64 + 64, rows] = nn(half, soft).astype(BF)
        return carry

    lax.fori_loop(0, IMGS, attend, 0)

    for i in range(IMGS):
        rows = pl.ds(i * TOK4, TOK4)
        y1 = y1_s[rows, :] + tn(mix_s[:, i * TOK4 : i * TOK4 + TOK4], mat4[:, 3 * C4 : 4 * C4])
        y1_s[rows, :] = y1
        n_s[rows, :] = (normalize(y1)[0] * norms[4:5] + norms[5:6]).astype(BF)

    def feed(j, carry):
        wide = pl.ds(pl.multiple_of(j * LC, LC), LC)
        w1 = mat4[:, pl.ds(pl.multiple_of(w1_at + j * LC, LC), LC)]
        for i in range(IMGS):
            rows = pl.ds(i * TOK4, TOK4)
            value = nn(n_s[rows, :], w1)
            hid_s[rows, wide] = value.astype(BF)
            store4(plain, moved, i, value)
        for lt in range(LC // 128):
            lanes = pl.ds(lt * 128, 128)
            out_lanes = pl.ds(pl.multiple_of(j * LC + lt * 128, 128), 128)
            kernel = depth[:, out_lanes]
            for i in range(IMGS):
                for qx in range(2):
                    total = None
                    for t, dy, dx in TAPS:
                        term = tap4(plain, moved, i, qx, dy, dx, lanes) * kernel[t : t + 1][None]
                        total = term if total is None else total + term
                    act, slope = gelu_both(total)
                    rows = pl.ds(i * TOK4 + qx * 128, 128)
                    act_s[rows, out_lanes] = act.reshape(128, 128).astype(BF)
                    slope_s[rows, out_lanes] = slope.reshape(128, 128).astype(BF)
        return carry

    lax.fori_loop(0, F4 // LC, feed, 0)

    pools = []
    hat_means = []
    for i in range(IMGS):
        rows = pl.ds(i * TOK4, TOK4)
        y2 = y1_s[rows, :] + nn(act_s[rows, :], tall4[4 * C3 :, :])
        y2_s[rows, :] = y2
        hat_mean = jnp.mean(normalize(y2)[0], axis=0, keepdims=True)
        hat_means.append(hat_mean)
        pools.append(hat_mean * norms[6:7] + norms[7:8])
    pooled = jnp.concatenate(pools + [jnp.zeros((8 - IMGS, C4), F32)], axis=0).astype(BF)
    logits = nn(pooled, mat4[:, wc_at:])

    row = lax.broadcasted_iota(jnp.int32, (8, CLASSES), 0)
    column = lax.broadcasted_iota(jnp.int32, (8, CLASSES), 1)
    target = jnp.full((8, CLASSES), -1, jnp.int32)
    present = jnp.zeros((8, CLASSES), F32)
    for i in range(IMGS):
        target = jnp.where(row == i, labels[i], target)
        present = jnp.where(row == i, valid[i].astype(F32), present)
    goal = (1.0 - SMOOTHING) * (column == target).astype(F32) + SMOOTHING / CLASSES
    shifted = logits - jnp.max(logits, axis=-1, keepdims=True)
    exponent = jnp.exp(shifted)
    mass = jnp.sum(exponent, axis=-1, keepdims=True)
    log_probs = shifted - jnp.log(mass)
    ce = -jnp.sum(goal * log_probs, axis=-1, keepdims=True)
    loss_o[...] = jnp.broadcast_to(jnp.sum(present[:, 0:1] * ce, axis=0, keepdims=True), (8, 128))
    dlogits = (present * inv_count[0] * (exponent / mass - goal)).astype(BF)

    gm_o[:, wc_at:] = tn(pooled, dlogits).astype(gm_o.dtype)
    dpool = nt(dlogits, mat4[:, wc_at:])
    dgain = None
    for i in range(IMGS):
        rows = pl.ds(i * TOK4, TOK4)
        one = dpool[i : i + 1]
        part = one * hat_means[i]
        dgain = part if dgain is None else dgain + part
        xhat, rstd = normalize(y2_s[rows, :])
        dy2 = norm_grad(jnp.broadcast_to(one * (1.0 / TOK4), (TOK4, C4)), xhat, rstd, norms[6:7])
        y2_s[rows, :] = dy2
    gn_o[6:7] = dgain
    gn_o[7:8] = column_sum(dpool)

    dy = y2_s[...].astype(BF)
    gt_o[4 * C3 :, :] = tn(act_s[...], dy).astype(gt_o.dtype)
    act_s[:, 0:C4] = dy
    act_s[:, C4 : 2 * C4] = jnp.zeros((IMGS * TOK4, C4), BF)
    gd_s[...] = jnp.zeros_like(gd_s)
    nt_val = n_s[...].T

    def feed_back(j, total):
        wide = pl.ds(pl.multiple_of(j * LC, LC), LC)
        w1_wide = pl.ds(pl.multiple_of(w1_at + j * LC, LC), LC)
        w2 = tall4[pl.ds(pl.multiple_of(4 * C3 + j * LC, LC), LC), :]
        for i in range(IMGS):
            rows = pl.ds(i * TOK4, TOK4)
            value = nt(act_s[rows, 0:C4], w2) * slope_s[rows, wide].astype(F32)
            store4(plain, moved, i, value)
        for lt in range(LC // 128):
            lanes = pl.ds(lt * 128, 128)
            out_lanes = pl.ds(pl.multiple_of(j * LC + lt * 128, 128), 128)
            kernel = depth[:, out_lanes]
            sums = [None] * 9
            for i in range(IMGS):
                for qx in range(2):
                    rows = pl.ds(i * TOK4 + qx * 128, 128)
                    base = hid_s[rows, out_lanes].astype(F32).reshape(16, 8, 128)
                    out = None
                    for t, dy, dx in TAPS:
                        value = tap4(plain, moved, i, qx, -dy, -dx, lanes)
                        term = value * kernel[t : t + 1][None]
                        out = term if out is None else out + term
                        part = jnp.sum(value * base, axis=0)
                        sums[t] = part if sums[t] is None else sums[t] + part
                    hid_s[rows, out_lanes] = out.reshape(128, 128).astype(BF)
            for t in range(9):
                gd_s[t, :, out_lanes] = sums[t]
        dhid = hid_s[:, wide]
        gm_o[:, w1_wide] = nn(nt_val, dhid).astype(gm_o.dtype)
        return carry_none

    carry_none = 0
    lax.fori_loop(0, F4 // LC, feed_back, 0)
    for t in range(9):
        gd_o[t : t + 1, :] = column_sum(gd_s[t])

    for ref_at in (2, 4, 0):
        pass
    dgain = dshift = None
    for i in range(IMGS):
        rows = pl.ds(i * TOK4, TOK4)
        dn = nt(hid_s[rows, :], mat4[:, w1_at : w1_at + F4])
        xhat, rstd = normalize(y1_s[rows, :])
        part_g, part_s = column_sum(dn * xhat), column_sum(dn)
        dgain = part_g if dgain is None else dgain + part_g
        dshift = part_s if dshift is None else dshift + part_s
        y2_s[rows, :] = y2_s[rows, :] + norm_grad(dn, xhat, rstd, norms[4:5])
    gn_o[4:5] = dgain
    gn_o[5:6] = dshift

    dprod = y2_s[...].astype(BF)
    gm_o[:, 3 * C4 : 4 * C4] = nn(mix_s[...], dprod).astype(gm_o.dtype)
    n_s[...] = nt(dprod, mat4[:, 3 * C4 : 4 * C4]).astype(BF)

    def attend_back(i, carry):
        rows = pl.ds(pl.multiple_of(i * TOK4, TOK4), TOK4)
        lane = lax.broadcasted_iota(jnp.int32, (TOK4, 128), 1)
        for pair in range(H4 // 2):
            at = pair * 128
            q = qkv_s[rows, at : at + 128]
            k = qkv_s[rows, C4 + at : C4 + at + 128]
            v = qkv_s[rows, 2 * C4 + at : 2 * C4 + at + 128]
            do = n_s[rows, at : at + 128]
            kt = k.T
            dqts, dks, dvs = [], [], []
            for half in range(2):
                soft = p_s[i * H4 + pair * 2 + half]
                dp = nt(half_of(v, half), do)
                wide_soft = soft.astype(F32)
                ds = wide_soft * (dp - jnp.sum(dp * wide_soft, axis=0, keepdims=True))
                ds = ds.astype(BF)
                dvs.append(nn(soft, do))
                dks.append(nn(ds, q))
                dqts.append(nn(kt[half * 64 : half * 64 + 64], ds))
            dqt = (jnp.concatenate(dqts, axis=0) * SCALE).astype(BF)
            qkv_s[rows, at : at + 128] = dqt.T
            qkv_s[rows, C4 + at : C4 + at + 128] = (jnp.where(lane < 64, dks[0], dks[1]) * SCALE).astype(BF)
            qkv_s[rows, 2 * C4 + at : 2 * C4 + at + 128] = jnp.where(lane < 64, dvs[0], dvs[1]).astype(BF)
        return carry

    lax.fori_loop(0, IMGS, attend_back, 0)
    ht = h_s[...].T
    for j in range(3):
        wide = slice(j * C4, j * C4 + C4)
        gm_o[:, wide] = nn(ht, qkv_s[:, wide]).astype(gm_o.dtype)

    sums = [None] * 4
    for i in range(IMGS):
        rows = pl.ds(i * TOK4, TOK4)
        dh = nt(qkv_s[rows, :], mat4[:, 0 : 3 * C4])
        hat0, rstd0 = normalize(first[rows, :])
        hat1, rstd1 = normalize(hat0 * norms[0:1] + norms[1:2])
        dy0 = y2_s[rows, :] + norm_grad(dh, hat1, rstd1, norms[2:3])
        dprod0 = norm_grad(dy0, hat0, rstd0, norms[0:1]).astype(BF)
        n_s[rows, :] = dprod0
        parts = [column_sum(dy0 * hat0), column_sum(dy0), column_sum(dh * hat1), column_sum(dh)]
        sums = [part if old is None else old + part for old, part in zip(sums, parts)]
        for plane in range(4):
            dx2_o[i, plane * 256 : plane * 256 + 256, :] = nt(dprod0, tall4[plane * C3 : plane * C3 + C3, :]).astype(BF)
    gn_o[0:4] = jnp.concatenate(sums, axis=0)
    for plane in range(4):
        total = None
        for i in range(IMGS):
            part = tn(x2[i, plane * 256 : plane * 256 + 256, :], n_s[i * TOK4 : i * TOK4 + TOK4, :])
            total = part if total is None else total + part
        gt_o[plane * C3 : plane * C3 + C3, :] = total.astype(gt_o.dtype)


def feed3_back(dx2, x1, n, hid, slope, act, tall3, mat3, depth, norms, dx1_o, g1_o, g2_o, gd_o, gn_o,
               acc1, acc2, accd, accn, plain, moved, dy_s, dyt_s, nt_s, da_s):
    step = pl.program_id(0)

    @pl.when(step == 0)
    def _():
        for ref in (plain, moved):
            ref[:, 0:1] = jnp.zeros((ref.shape[0], 1, 8, LC), F32)
            ref[:, 17:18] = jnp.zeros((ref.shape[0], 1, 8, LC), F32)
        for ref in (acc1, acc2, accd, accn):
            ref[...] = jnp.zeros_like(ref)

    dy = dx2[0]
    dy_s[...] = dy
    dyt_s[...] = dy.T
    nt_s[...] = n[0].T

    def chunk(j, carry):
        wide = pl.ds(pl.multiple_of(j * LC, LC), LC)
        w2 = tall3[pl.ds(pl.multiple_of(PATCH + 4 * C3 + j * LC, LC), LC), :]
        for plane in range(4):
            rows = pl.ds(plane * 256, 256)
            value = nt(dy_s[rows, :], w2) * slope[0, rows, wide].astype(F32)
            store3(plain, moved, plane, value)
        for lt in range(LC // 128):
            lanes = pl.ds(lt * 128, 128)
            out_lanes = pl.ds(pl.multiple_of(j * LC + lt * 128, 128), 128)
            kernel = depth[:, out_lanes]
            sums = [None] * 9
            for py in range(2):
                for xm in range(4):
                    rows = pl.ds(class3(py, xm) * 128, 128)
                    base = hid[0, rows, out_lanes].astype(F32).reshape(16, 8, 128)
                    out = None
                    for t, dy, dx in TAPS:
                        value = tap3(plain, moved, py, xm, -dy, -dx, lanes)
                        term = value * kernel[t : t + 1][None]
                        out = term if out is None else out + term
                        part = jnp.sum(value * base, axis=0)
                        sums[t] = part if sums[t] is None else sums[t] + part
                    da_s[rows, out_lanes] = out.reshape(128, 128).astype(BF)
            for t in range(9):
                accd[t, :, out_lanes] += sums[t]
        da = da_s[:, wide]
        acc1[:, wide] += nn(nt_s[...], da)
        acc2[:, wide] += nn(dyt_s[...], act[0, :, wide])
        return carry

    lax.fori_loop(0, F3 // LC, chunk, 0)
    for b in range(4):
        rows = pl.ds(b * 256, 256)
        dn = nt(da_s[rows, :], mat3[:, 4 * C3P :])
        xhat, rstd = normalize(x1[0, rows, :])
        accn[0:1] += column_sum(dn * xhat)
        accn[1:2] += column_sum(dn)
        dx1_o[0, rows, :] = dx2[0, rows, :].astype(F32) + norm_grad(dn, xhat, rstd, norms[6:7])

    @pl.when(step == IMGS - 1)
    def _():
        g1_o[...] = acc1[...].astype(g1_o.dtype)
        g2_o[...] = acc2[...].T.astype(g2_o.dtype)
        gn_o[...] = accn[...]
        for t in range(9):
            gd_o[t : t + 1, :] = column_sum(accd[t])


def attend3_back(dx1, z, h, red, q, k, v, p, mix, patches, tall3, mat3, norms, ge_o, gr_o, gm_o, gn_o,
                 acce, accr, accq, acck, accv, acco, accn, dk_s, dv_s, kt_s, dqt_s, dr_s):
    step = pl.program_id(0)

    @pl.when(step == 0)
    def _():
        for ref in (acce, accr, accq, acck, accv, acco, accn):
            ref[...] = jnp.zeros_like(ref)

    kt_s[...] = k[0].T
    dk_s[...] = jnp.zeros_like(dk_s)
    dv_s[...] = jnp.zeros_like(dv_s)
    wo = mat3[0:C3, 3 * C3P : 3 * C3P + C3]
    lane = lax.broadcasted_iota(jnp.int32, (256, 128), 1)

    def queries(b, carry):
        rows = pl.ds(pl.multiple_of(b * 256, 256), 256)
        dprod = dx1[0, rows, :].astype(BF)
        acco[...] += nn(mix[0, :, rows], dprod)
        dmix = nt(dprod, wo).astype(BF)
        dmix = jnp.concatenate([dmix, jnp.zeros((256, C3P - C3), BF)], axis=1)
        for pair in range(3):
            lanes = slice(pair * 128, pair * 128 + 128)
            do = dmix[:, lanes]
            qp = q[0, rows, lanes]
            dks, dvs = [], []
            for half in range(2 if pair < 2 else 1):
                head = pair * 2 + half
                soft = p[0, head, :, rows]
                dp = nt(half_of(v[0, :, lanes], half), do)
                wide_soft = soft.astype(F32)
                ds = wide_soft * (dp - jnp.sum(dp * wide_soft, axis=0, keepdims=True))
                ds = ds.astype(BF)
                dvs.append(nn(soft, do))
                dks.append(nn(ds, qp))
                dqt = nn(kt_s[head * 64 : head * 64 + 64, :], ds) * SCALE
                dqt_s[head * 64 : head * 64 + 64, rows] = dqt.astype(BF)
            if len(dks) == 2:
                dk_s[:, lanes] += jnp.where(lane < 64, dks[0], dks[1])
                dv_s[:, lanes] += jnp.where(lane < 64, dvs[0], dvs[1])
            else:
                dk_s[:, lanes] += dks[0]
                dv_s[:, lanes] += dvs[0]
        return carry

    lax.fori_loop(0, 4, queries, 0)

    dk = (dk_s[...] * SCALE).astype(BF)
    dv = dv_s[...].astype(BF)
    hat_r, rstd_r = normalize(red[0])
    r = (hat_r * norms[4:5] + norms[5:6]).astype(BF)
    acck[...] += tn(r, dk)
    accv[...] += tn(r, dv)
    dr = nt(dk, mat3[:, C3P : 2 * C3P]) + nt(dv, mat3[:, 2 * C3P : 3 * C3P])
    accn[4:5] += column_sum(dr * hat_r)
    accn[5:6] += column_sum(dr)
    dred = norm_grad(dr, hat_r, rstd_r, norms[4:5]).astype(BF)
    accq[...] += nn(dqt_s[...], h[0])
    for b in range(4):
        rows = pl.ds(b * 256, 256)
        wr = tall3[PATCH + C3 * b : PATCH + C3 * (b + 1)]
        accr[C3 * b : C3 * (b + 1)] += tn(h[0, rows, :], dred)
        dh = tn(dqt_s[:, rows], mat3[:, 0:C3].T) + nt(dred, wr)
        hat0, rstd0 = normalize(z[0, rows, :])
        hat1, rstd1 = normalize(hat0 * norms[0:1] + norms[1:2])
        accn[2:3] += column_sum(dh * hat1)
        accn[3:4] += column_sum(dh)
        dx0 = dx1[0, rows, :] + norm_grad(dh, hat1, rstd1, norms[2:3])
        accn[0:1] += column_sum(dx0 * hat0)
        accn[1:2] += column_sum(dx0)
        dz = norm_grad(dx0, hat0, rstd0, norms[0:1]).astype(BF)
        acce[...] += tn(dz, patches[0, rows, :])

    @pl.when(step == IMGS - 1)
    def _():
        ge_o[...] = acce[...].T.astype(ge_o.dtype)
        gr_o[...] = accr[...].astype(gr_o.dtype)
        gm_o[:, 0:C3] = accq[...].T.astype(gm_o.dtype)
        gm_o[:, C3P : 2 * C3P] = acck[...].astype(gm_o.dtype)
        gm_o[:, 2 * C3P : 3 * C3P] = accv[...].astype(gm_o.dtype)
        gm_o[:, 3 * C3P : 3 * C3P + C3] = acco[...].astype(gm_o.dtype)
        gn_o[...] = accn[...]


def whole(shape, dtype=None):
    return pl.BlockSpec(shape, lambda i: (0,) * len(shape), pipeline_mode=pl.Buffered(1))


def per_image(*shape):
    return pl.BlockSpec((1,) + shape, lambda i: (i,) + (0,) * len(shape))


def sds(*shape, dtype=F32):
    return jax.ShapeDtypeStruct(shape, dtype)


PARAMS = pltpu.CompilerParams(vmem_limit_bytes=VMEM_BYTES, dimension_semantics=("arbitrary",))


def run_embed_attend(patches, tall3, mat3, norms3):
    return pl.pallas_call(
        embed_attend,
        grid=(IMGS,),
        in_specs=[per_image(TOK3, PATCH), whole(tall3.shape), whole(mat3.shape), whole(norms3.shape)],
        out_specs=[
            per_image(TOK3, C3), per_image(TOK3, C3), per_image(256, C3), per_image(TOK3, C3P), per_image(256, C3P),
            per_image(256, C3P), per_image(H3, 256, TOK3), per_image(C3, TOK3), per_image(TOK3, C3),
        ],
        out_shape=[
            sds(IMGS, TOK3, C3), sds(IMGS, TOK3, C3, dtype=BF), sds(IMGS, 256, C3), sds(IMGS, TOK3, C3P, dtype=BF),
            sds(IMGS, 256, C3P, dtype=BF), sds(IMGS, 256, C3P, dtype=BF), sds(IMGS, H3, 256, TOK3, dtype=BF),
            sds(IMGS, C3, TOK3, dtype=BF), sds(IMGS, TOK3, C3),
        ],
        scratch_shapes=[pltpu.VMEM((TOK3, C3), F32), pltpu.VMEM((C3P, 256), BF)],
        compiler_params=PARAMS,
        name="embed_attend",
    )(patches, tall3, mat3, norms3)


def run_feed3(x1, tall3, mat3, depth, norms3):
    return pl.pallas_call(
        feed3,
        grid=(IMGS,),
        in_specs=[per_image(TOK3, C3), whole(tall3.shape), whole(mat3.shape), whole(depth.shape), whole(norms3.shape)],
        out_specs=[per_image(TOK3, C3), per_image(TOK3, F3), per_image(TOK3, F3), per_image(TOK3, F3), per_image(TOK3, C3)],
        out_shape=[
            sds(IMGS, TOK3, C3, dtype=BF), sds(IMGS, TOK3, F3, dtype=BF), sds(IMGS, TOK3, F3, dtype=BF),
            sds(IMGS, TOK3, F3, dtype=BF), sds(IMGS, TOK3, C3, dtype=BF),
        ],
        scratch_shapes=[pltpu.VMEM((8, 18, 8, LC), F32), pltpu.VMEM((4, 18, 8, LC), F32)],
        compiler_params=PARAMS,
        name="feed3",
    )(x1, tall3, mat3, depth, norms3)


def run_section4(labels, valid, inv_count, x2, mat4, tall4, depth, norms4):
    vm = pl.BlockSpec(memory_space=pltpu.VMEM)
    sm = pl.BlockSpec(memory_space=pltpu.SMEM)
    rows = IMGS * TOK4
    return pl.pallas_call(
        section4,
        in_specs=[sm, sm, sm, vm, vm, vm, vm, vm],
        out_specs=[vm] * 6,
        out_shape=[
            sds(IMGS, TOK3, C3, dtype=BF), sds(*mat4.shape, dtype=BF), sds(*tall4.shape, dtype=BF), sds(9, F4), sds(8, C4),
            sds(8, 128),
        ],
        scratch_shapes=[
            pltpu.VMEM((rows, C4), F32), pltpu.VMEM((rows, C4), F32), pltpu.VMEM((rows, C4), F32),
            pltpu.VMEM((rows, C4), BF), pltpu.VMEM((rows, 3 * C4), BF), pltpu.VMEM((IMGS * H4, 256, 256), BF),
            pltpu.VMEM((C4, rows), BF), pltpu.VMEM((rows, C4), BF), pltpu.VMEM((rows, F4), BF),
            pltpu.VMEM((rows, F4), BF), pltpu.VMEM((rows, F4), BF), pltpu.VMEM((IMGS, 2, 18, 8, LC), F32),
            pltpu.VMEM((IMGS, 2, 18, 8, LC), F32), pltpu.VMEM((9, 8, F4), F32),
        ],
        compiler_params=pltpu.CompilerParams(vmem_limit_bytes=VMEM_BYTES),
        name="section4",
    )(labels, valid, inv_count, x2, mat4, tall4, depth, norms4)


def run_feed3_back(dx2, x1, n, hid, slope, act, tall3, mat3, depth, norms3):
    return pl.pallas_call(
        feed3_back,
        grid=(IMGS,),
        in_specs=[
            per_image(TOK3, C3), per_image(TOK3, C3), per_image(TOK3, C3), per_image(TOK3, F3), per_image(TOK3, F3),
            per_image(TOK3, F3), whole(tall3.shape), whole(mat3.shape), whole(depth.shape), whole(norms3.shape),
        ],
        out_specs=[per_image(TOK3, C3), whole((C3, F3)), whole((F3, C3)), whole((9, F3)), whole((2, C3))],
        out_shape=[sds(IMGS, TOK3, C3), sds(C3, F3, dtype=BF), sds(F3, C3, dtype=BF), sds(9, F3), sds(2, C3)],
        scratch_shapes=[
            pltpu.VMEM((C3, F3), F32), pltpu.VMEM((C3, F3), F32), pltpu.VMEM((9, 8, F3), F32), pltpu.VMEM((2, C3), F32),
            pltpu.VMEM((8, 18, 8, LC), F32), pltpu.VMEM((4, 18, 8, LC), F32), pltpu.VMEM((TOK3, C3), BF),
            pltpu.VMEM((C3, TOK3), BF), pltpu.VMEM((C3, TOK3), BF), pltpu.VMEM((TOK3, F3), BF),
        ],
        compiler_params=PARAMS,
        name="feed3_back",
    )(dx2, x1, n, hid, slope, act, tall3, mat3, depth, norms3)


def run_attend3_back(dx1, z, h, red, q, k, v, p, mix, patches, tall3, mat3, norms3):
    return pl.pallas_call(
        attend3_back,
        grid=(IMGS,),
        in_specs=[
            per_image(TOK3, C3), per_image(TOK3, C3), per_image(TOK3, C3), per_image(256, C3), per_image(TOK3, C3P),
            per_image(256, C3P), per_image(256, C3P), per_image(H3, 256, TOK3), per_image(C3, TOK3),
            per_image(TOK3, PATCH), whole(tall3.shape), whole(mat3.shape), whole(norms3.shape),
        ],
        out_specs=[whole((PATCH, C3)), whole((4 * C3, C3)), whole((C3, 4 * C3P)), whole((6, C3))],
        out_shape=[sds(PATCH, C3, dtype=BF), sds(4 * C3, C3, dtype=BF), sds(C3, 4 * C3P, dtype=BF), sds(6, C3)],
        scratch_shapes=[
            pltpu.VMEM((C3, PATCH), F32), pltpu.VMEM((4 * C3, C3), F32), pltpu.VMEM((C3, C3), F32),
            pltpu.VMEM((C3, C3P), F32), pltpu.VMEM((C3, C3P), F32), pltpu.VMEM((C3, C3), F32), pltpu.VMEM((6, C3), F32),
            pltpu.VMEM((256, C3P), F32), pltpu.VMEM((256, C3P), F32), pltpu.VMEM((C3P, 256), BF),
            pltpu.VMEM((C3, TOK3), BF), pltpu.VMEM((256, C3), F32),
        ],
        compiler_params=PARAMS,
        name="attend3_back",
    )(dx1, z, h, red, q, k, v, p, mix, patches, tall3, mat3, norms3)


def pad_mat3(mat):
    pieces = [mat[:, at * C3 : at * C3 + C3] for at in range(4)]
    pieces = [jnp.pad(piece, ((0, 0), (0, C3P - C3))) for piece in pieces]
    return jnp.concatenate(pieces + [mat[:, 4 * C3 :]], axis=1)


def reorder(patches):
    count = patches.shape[0]
    grid = patches.reshape(count, 16, 2, 8, 2, 2, patches.shape[-1])
    return grid.transpose(0, 2, 5, 4, 1, 3, 6).reshape(patches.shape)


def local_gradients(patches, labels, valid, inv_count, mat3, tall3, mat4, tall4, depth, norms3, norms4):
    z, h, red, q, k, v, p, mix, x1 = run_embed_attend(patches, tall3, mat3, norms3)
    n, hid, slope, act, x2 = run_feed3(x1, tall3, mat3, depth[:, :F3], norms3)
    dx2, gm4, gt4, gd4, gn4, loss = run_section4(labels, valid, inv_count, x2, mat4, tall4, depth[:, F3:], norms4)
    dx1, g1, g2, gd3, gn3b = run_feed3_back(dx2, x1, n, hid, slope, act, tall3, mat3, depth[:, :F3], norms3)
    ge, gr, gm3, gn3a = run_attend3_back(dx1, z, h, red, q, k, v, p, mix, patches, tall3, mat3, norms3)
    return loss, gm4, gt4, gd4, gn4, g1, g2, gd3, gn3b, ge, gr, gm3, gn3a


def adamw(master, moment, second, gradient, is_norm):
    step_rate = 0.5 if is_norm else 0.05
    decay_now = 0.0 if is_norm else 0.05
    first = 0.9 * moment + 0.1 * gradient
    second_new = 0.999 * second + 0.001 * gradient * gradient
    first_hat = first / (1.0 - 0.9**STEP)
    second_hat = second_new / (1.0 - 0.999**STEP)
    updated = master - step_rate * (first_hat / (jnp.sqrt(second_hat) + 1e-08) + decay_now * master)
    return (updated, first, second_new)


def body(patches, labels, valid, *state):
    masters, moments, seconds = state[0:7], state[7:14], state[14:21]
    both = ("dp", "fsdp")
    image_count = lax.psum(jnp.sum(valid).astype(F32), both)
    inv_count = (1.0 / image_count).reshape(1)

    mat3, tall3, mat4, tall4, depth, norms3, norms4 = [master.astype(BF) for master in masters]
    small = [jnp.pad(piece.T, ((0, 0), (0, 16 - piece.shape[0]))) for piece in (depth, norms3, norms4)]
    sizes = [piece.shape[0] for piece in small]
    small = lax.all_gather(jnp.concatenate(small, axis=0), "fsdp", axis=0)
    edges = [0, sizes[0], sizes[0] + sizes[1], sum(sizes)]
    parts = [small[:, edges[at] : edges[at + 1]].reshape(-1, 16).T.astype(F32) for at in range(3)]
    depth_all, norms3_all, norms4_all = parts[0][:9], parts[1][:8], parts[2][:8]
    tall3_all = lax.all_gather(tall3, "fsdp", axis=0, tiled=True)
    mat3_all = lax.all_gather(pad_mat3(mat3), "fsdp", axis=0, tiled=True)
    tall4_all = lax.all_gather(tall4, "fsdp", axis=0, tiled=True)
    mat4_all = lax.all_gather(mat4, "fsdp", axis=0, tiled=True)

    loss, gm4, gt4, gd4, gn4, g1, g2, gd3, gn3b, ge, gr, gm3, gn3a = local_gradients(
        reorder(patches.reshape(IMGS, TOK3, PATCH)), labels.reshape(IMGS), valid.reshape(IMGS), inv_count,
        mat3_all, tall3_all, mat4_all, tall4_all, depth_all, norms3_all, norms4_all,
    )

    def share(piece):
        return lax.psum(lax.psum_scatter(piece, "fsdp", scatter_dimension=0, tiled=True).astype(F32), "dp")

    grad_mat4 = share(gm4)
    grad_tall4 = share(gt4)
    grad_feed = share(g1)
    grad_mix = share(gm3)
    grad_tall3 = share(jnp.concatenate([ge, gr, g2], axis=0))
    grad_mat3 = jnp.concatenate([grad_mix[:, at * C3P : at * C3P + C3] for at in range(4)] + [grad_feed], axis=1)
    flat = [gd3.reshape(-1), gd4.reshape(-1), gn3a.reshape(-1), gn3b.reshape(-1), gn4.reshape(-1)]
    flat = lax.psum(jnp.concatenate(flat), both)
    me = lax.axis_index("fsdp")
    ends = [0]
    for size in (9 * F3, 9 * F4, 6 * C3, 2 * C3, 8 * C4):
        ends.append(ends[-1] + size)
    cut = [flat[ends[at] : ends[at + 1]] for at in range(5)]
    full = [
        jnp.concatenate([cut[0].reshape(9, F3), cut[1].reshape(9, F4)], axis=1),
        jnp.concatenate([cut[2].reshape(6, C3), cut[3].reshape(2, C3)], axis=0),
        cut[4].reshape(8, C4),
    ]
    own = [
        lax.dynamic_slice_in_dim(piece, me * master.shape[1], master.shape[1], 1)
        for piece, master in zip(full, masters[4:])
    ]
    group = [grad_mat3, grad_tall3, grad_mat4, grad_tall4] + own

    square = jnp.float32(0.0)
    for shard in group:
        square = square + jnp.sum(shard * shard)
    dp_count = lax.axis_size("dp")
    totals = lax.psum(jnp.stack([square / dp_count, loss[0, 0]]), both)
    grad_norm = jnp.sqrt(totals[0])
    clip_factor = jnp.minimum(1.0, CLIP_LEVEL / (grad_norm + 1e-06))
    results = [
        adamw(masters[at], moments[at], seconds[at], clip_factor * group[at], at >= 5) for at in range(7)
    ]
    return (
        *[result[0] for result in results],
        *[result[1] for result in results],
        *[result[2] for result in results],
        totals[1],
        image_count,
        grad_norm,
    )


def solution(mesh):
    rows, columns = P("fsdp", None), P(None, "fsdp")
    weights = (rows,) * 4 + (columns,) * 3
    images = P(None, ("dp", "fsdp"))
    in_specs = (P(None, ("dp", "fsdp"), None, None), images, images) + weights * 3
    out_specs = weights * 3 + (P(), P(), P())
    return jax.shard_map(body, mesh=mesh, in_specs=in_specs, out_specs=out_specs, check_vma=False)
```

time: 2170 us -> 976 us (0.45)
  other arithmetic: 721 us -> 28.3 us
  matrix products: 580 us -> 0 us
  Pallas kernels: 0 us -> 324 us
  local copies, waits for them, and re-layouts: 362 us -> 41.9 us
  blocking collectives: 125 us -> 207 us
  waiting for transfers between devices: 305 us -> 347 us
  between operations: 56.3 us -> 22.7 us
    dot_general x304 -> x0, matrix products: 548 us -> none  [the longest x248 483 us: matmul(): return jnp.dot(left, right, preferred_element_type=jnp.float32)]
    pallas_call x0 -> x5, Pallas kernels: none -> 324 us  [the longest x1 88.3 us: run_section4(): pl.pallas_call(section4, in_specs=[sm, sm, sm, vm, vm, vm, vm, vm], out_s...]
    add x17 -> x0, other arithmetic: 224 us -> none  [the longest x10 191 us: depthwise(): total + padded[offset // 3:offset // 3 + row_count, offset % 3:offset % 3...]
    reshape x96 -> x9, local copies, waits for them, and re-layouts: 179 us -> 3.69 us  [the longest x1 0.92 us: body(): gd4.reshape(-1)]
    convert_element_type x121 -> x5, other arithmetic: 137 us -> 3.62 us  [the longest x4 3.6 us: body(): master.astype(BF)]
    psum x3, blocking collectives: 74.2 us -> 197 us  [the longest x1 117 us: share(): lax.psum(lax.psum_scatter(piece, 'fsdp', scatter_dimension=0, tiled=True)...]
    reduce_sum x167 -> x8, other arithmetic: 129 us -> 7.64 us  [the longest x7 7.01 us: body(): square = square + jnp.sum(shard * shard)]
    reduce_scatter x3 -> x5, waiting for transfers between devices: 125 us -> 231 us  [share(): lax.psum_scatter(piece, 'fsdp', scatter_dimension=0, tiled=True).astype(F32)]
  transfers between devices with their start and end apart: 11 -> 10, of which waited for: 6 -> 6; matrix products, arithmetic and copies ran while one was open for 18% -> 4% of each run, Pallas kernels for 0% -> 11%
where the time goes in v1:
time: 976 us; the launch traced here: 972 us
  waiting for transfers between devices  347 us (36%)
  Pallas kernels  324 us (33%)
  blocking collectives  207 us (21%)
  local copies, waits for them, and re-layouts  41.9 us (4%)
  other arithmetic  28.3 us (3%)
  between operations  22.7 us (2%)
    reduce_scatter x5, waiting for transfers between devices, share(): lax.psum_scatter(piece, 'fsdp', scatter_dimension=0, tiled=True).astype(F32)  231 us
    psum x1, blocking collectives, share(): lax.psum(lax.psum_scatter(piece, 'fsdp', scatter_dimension=0, tiled=True)...  117 us
    psum x1, waiting for transfers between devices, body(): flat = lax.psum(jnp.concatenate(flat), both)  113 us
    pallas_call x1, Pallas kernels, run_section4(): pl.pallas_call(section4, in_specs=[sm, sm, sm, vm, vm, vm, vm, vm], out_s...  88.3 us
    pallas_call x1, Pallas kernels, run_feed3_back(): pl.pallas_call(feed3_back, grid=(IMGS,), in_specs=[per_image(TOK3, C3), p...  68.2 us
    pallas_call x1, Pallas kernels, run_attend3_back(): pl.pallas_call(attend3_back, grid=(IMGS,), in_specs=[per_image(TOK3, C3),...  62.8 us
    pallas_call x1, Pallas kernels, run_embed_attend(): pl.pallas_call(embed_attend, grid=(IMGS,), in_specs=[per_image(TOK3, PATC...  57.9 us
    pallas_call x1, Pallas kernels, run_feed3(): pl.pallas_call(feed3, grid=(IMGS,), in_specs=[per_image(TOK3, C3), whole(...  46.7 us
  transfers between devices with their start and end apart: 10, of which 6 were waited for; matrix products, arithmetic and copies ran while one was open for 4% of the time, Pallas kernels for 11%

profile of v1, /device:TPU:0, one launch (start us, length us, event | category | flops | bytes accessed | tf_op | source)
XLA Modules:
  0.0 971.5 jit_solution(420597798558526006)
XLA Ops:
  7.3 1.1 convert_element_type.75
  8.5 0.7 fusion.10
  9.2 0.7 copy-done.15
  10.0 0.8 convert_element_type.74
  10.9 0.8 convert_element_type.85
  11.8 0.9 convert_element_type.84
  12.8 0.6 reduce_sum.72
  14.1 42.0 %psum.56 = f32[]{:T(128)} all-reduce(f32[]{:T(128)S(6)} %convert_element_type.73), channel_id=1, replica_groups=mesh['dp'=4,'fsdp'=8] {'dp','fsdp'}, use_global_device_ids=true, to_apply=%region_1.0 | all-reduce | flops 1 | bytes 8 | tf_op jit(solution)/shard_map/psum | solution.py:754
  56.3 10.2 %all-gather.1 = bf16[8,520,16]{1,2,0:T(8,128)(2,1)S(1)} all-gather(bf16[1,520,16]{1,2,0:T(8,128)(2,1)S(1)} %fusion.13), channel_id=2, replica_groups=mesh['dp'=4,'fsdp'=8] {'fsdp'}, dimensions={0}, use_global_device_ids=true | all-gather | bytes 149760 | tf_op jit(solution)/shard_map/all_gather | solution.py:760
  66.8 0.6 slice.115.depth
  67.5 0.7 slice.116.depth
  68.4 13.5 %reshape_reshape.3 = bf16[4,16,2,8,2,2,768]{6,5,4,3,2,1,0:T(2,128)(2,1)} reshape(bf16[4,1,1024,768]{3,2,1,0:T(8,128)(2,1)} %param.24) | data formatting | bytes 12582912 | tf_op jit(solution)/shard_map/reshape;reshape | solution.py:727
  81.8 6.8 copy.52
  89.4 0.6 slice_convert_fusion.2.norms
  90.0 0.6 slice_convert_fusion.1.norms
  90.6 57.9 %embed_attend.1 = (f32[4,1024,320]{2,1,0:T(8,128)}, bf16[4,1024,320]{2,1,0:T(8,128)(2,1)}, f32[4,256,320]{2,1,0:T(8,128)}, bf16[4,1024,384]{2,1,0:T(8,128)(2,1)}...) custom-call(bf16[4,1024,768]{2,1,0:T(8,128)(2,1)} %bitcast.31, ...), custom_call_target="tpu_custom_call" | custom-call | tf_op jit(solution)/shard_map/embed_attend/pallas_call | solution.py:618
  148.6 46.7 %feed3.1 = (bf16[4,1024,320]{2,1,0:T(8,128)(2,1)}, bf16[4,1024,1280]{2,1,0:T(8,128)(2,1)}, bf16[4,1024,1280]{2,1,0:T(8,128)(2,1)}, bf16[4,1024,1280]{2,1,0:T(8,128)(2,1)}, bf16[4,1024,320]{2,1,0:T(8,128)(2,1)}) custom-call(f32[4,1024,320]{2,1,0:T(8,128)} %get-tuple-element.53.x1, bf16[3328,320]{1,0:T(8,128)(2,1)} %all-gather.7.cloned.1.call-done.tall3, ...), custom_call_target="tpu_custom_call" | custom-call | tf_op jit(solution)/shard_map/feed3/pallas_call | solution.py:638
  195.4 88.3 %section4.1 = (bf16[4,1024,320]{2,1,0:T(8,128)(2,1)}, bf16[512,5096]{1,0:T(8,128)(2,1)}, bf16[3328,512]{1,0:T(8,128)(2,1)}, f32[9,2048]{1,0:T(8,128)}, f32[8,512]{1,0:T(8,128)}, /*index=5*/f32[8,128]{1,0:T(8,128)}) custom-call(s32[4]{0:T(128)} %bitcast.39, s32[4]{0:T(128)} %bitcast.40, f32[1]{0:T(128)} %bitcast.2.inv_count, ...), custom_call_target="tpu_custom_call" | custom-call | tf_op jit(solution)/shard_map/section4/pallas_call | solution.py:657
  283.6 68.2 %feed3_back.1 = (f32[4,1024,320]{2,1,0:T(8,128)}, bf16[320,1280]{1,0:T(8,128)(2,1)}, bf16[1280,320]{1,0:T(8,128)(2,1)}, f32[9,1280]{1,0:T(8,128)}, f32[2,320]{1,0:T(2,128)}) custom-call(bf16[4,1024,320]{2,1,0:T(8,128)(2,1)} %get-tuple-element.55.dx2, f32[4,1024,320]{2,1,0:T(8,128)} %get-tuple-element.53.x1, bf16[4,1024,320]{2,1,0:T(8,128)(2,1)} %get-tuple-element.56.n, ...), custom_call_target="tpu_custom_call" | custom-call | tf_op jit(solution)/shard_map/feed3_back/pallas_call | solution.py:678
  351.8 0.9 reshape.104
  352.7 0.9 reshape.105
  353.7 62.8 %attend3_back.1 = (bf16[768,320]{1,0:T(8,128)(2,1)}, bf16[1280,320]{1,0:T(8,128)(2,1)}, bf16[320,1536]{1,0:T(8,128)(2,1)}, f32[6,320]{1,0:T(8,128)}) custom-call(f32[4,1024,320]{2,1,0:T(8,128)} %get-tuple-element.60.dx1, f32[4,1024,320]{2,1,0:T(8,128)} %get-tuple-element.61.z, bf16[4,1024,320]{2,1,0:T(8,128)(2,1)} %get-tuple-element.62.h, ...), custom_call_target="tpu_custom_call" | custom-call | tf_op jit(solution)/shard_map/attend3_back/pallas_call | solution.py:698
  416.5 0.9 reshape.106
  417.4 0.8 reshape.107
  418.2 0.7 copy.56
  418.9 1.4 constant_dynamic-update-slice_fusion
  420.3 1.5 constant_dynamic-update-slice_fusion.4
  421.9 1.3 constant_dynamic-update-slice_fusion.3
  423.2 1.3 constant_dynamic-update-slice_fusion.2
  424.5 1.3 constant_dynamic-update-slice_fusion.1
  426.5 0.7 reduce-scatter.6.cloned.1.call-update
  427.2 2.8 pad_maximum_fusion
  430.1 0.7 reduce-scatter.14.cloned.1.call-update
  431.4 1.2 slice.104
  432.6 113.2 %all-reduce.10.cloned.1.call-done = f32[36608]{0:T(1024)} async-done(((f32[36608]{0:T(1024)}), f32[36608]{0:T(1024)}) %all-reduce.10.cloned.1.call-update) | async-done | bytes 146448 | tf_op jit(solution)/shard_map/psum | solution.py:784
  545.7 0.7 slice.125
  546.5 0.7 slice.126
  547.3 0.9 slice.124
  548.2 0.8 slice.123
  549.0 0.7 slice.127
  549.8 0.7 multiply_reduce_fusion.5
  550.4 0.7 multiply_reduce_fusion.6
  551.1 1.3 multiply_reduce_fusion.4
  552.4 33.6 %reduce-scatter.8.cloned.1.call-done = bf16[40,1280]{1,0:T(8,128)(2,1)} async-done(((bf16[320,1280]{1,0:T(8,128)(2,1)}), bf16[40,1280]{1,0:T(8,128)(2,1)}) %reduce-scatter.8.cloned.1.call-update) | async-done | bytes 102416 | tf_op jit(solution)/shard_map/reduce_scatter | solution.py:775
  586.0 39.9 %reduce-scatter.6.cloned.1.call-done = bf16[40,1536]{1,0:T(8,128)(2,1)} async-done(((bf16[320,1536]{1,0:T(8,128)(2,1)}), bf16[40,1536]{1,0:T(8,128)(2,1)}) %reduce-scatter.6.cloned.1.call-update) | async-done | bytes 122896 | tf_op jit(solution)/shard_map/reduce_scatter | solution.py:775
  625.9 46.8 %reduce-scatter.10.cloned.1.call-done = bf16[416,320]{1,0:T(8,128)(2,1)} async-done(((bf16[3328,320]{1,0:T(8,128)(2,1)}), bf16[416,320]{1,0:T(8,128)(2,1)}) %reduce-scatter.10.cloned.1.call-update) | async-done | bytes 266256 | tf_op jit(solution)/shard_map/reduce_scatter | solution.py:775
  672.7 51.4 %reduce-scatter.14.cloned.1.call-done = bf16[416,512]{1,0:T(8,128)(2,1)} async-done(((bf16[3328,512]{1,0:T(8,128)(2,1)}), bf16[416,512]{1,0:T(8,128)(2,1)}) %reduce-scatter.14.cloned.1.call-update) | async-done | bytes 426000 | tf_op jit(solution)/shard_map/reduce_scatter | solution.py:775
  724.0 59.8 %reduce-scatter.12.cloned.1.call-done = bf16[64,5096]{1,0:T(8,128)(2,1)} async-done(((bf16[512,5096]{1,0:T(8,128)(2,1)}), bf16[64,5096]{1,0:T(8,128)(2,1)}) %reduce-scatter.12.cloned.1.call-update) | async-done | bytes 652304 | tf_op jit(solution)/shard_map/reduce_scatter | solution.py:775
  783.8 116.6 %all-reduce.11 = (f32[40,1536]{1,0:T(8,128)S(1)}, f32[40,1280]{1,0:T(8,128)}, f32[416,320]{1,0:T(8,128)}, f32[64,5096]{1,0:T(8,128)S(1)}, f32[416,512]{1,0:T(8,128)S(1)}) all-reduce(bf16[40,1536]{1,0:T(8,128)(2,1)} %reduce-scatter.6.cloned.1.call-done, ...), channel_id=1, replica_groups=mesh['dp'=4,'fsdp'=8] {'dp'}, use_global_device_ids=true, to_apply=%region_3.4 | all-reduce | flops 784896 | bytes 4709376 | tf_op jit(solution)/shard_map/psum | solution.py:775
  900.4 0.7 fusion.26
  901.1 1.1 concatenate.23
  902.2 0.7 multiply_reduce_fusion.3
  902.9 1.9 multiply_reduce_fusion.2
  904.8 0.9 multiply_reduce_fusion
  905.7 0.8 multiply_reduce_fusion.1
  911.1 0.7 pad_maximum_fusion.1
  911.8 38.3 %psum.63 = f32[2]{0:T(128)S(1)} all-reduce(f32[2]{0:T(128)S(1)} %pad_maximum_fusion.1), channel_id=1, replica_groups=mesh['dp'=4,'fsdp'=8] {'dp','fsdp'}, use_global_device_ids=true, to_apply=%region_20.21 | all-reduce | flops 2 | bytes 16 | tf_op jit(solution)/shard_map/psum | solution.py:805
  951.5 1.4 multiply_subtract_fusion.5
  952.9 3.5 multiply_subtract_fusion.1
  956.4 2.6 multiply_subtract_fusion
  959.1 1.6 multiply_subtract_fusion.2
  960.7 1.2 multiply_subtract_fusion.3
  962.0 0.6 multiply_subtract_fusion.6
  962.6 0.7 multiply_subtract_fusion.4
  (106 shorter events, 3.5 us)
Async XLA Ops:
  7.2 2.8 copy-start.3
  7.2 3.6 copy-start.2
  7.2 83.4 %all-gather.9.cloned.1.call-start = ((), (), s32[]{:S(2)}) async-start(), calls=%async_computation.6 | async-start | bytes 2027520 | tf_op jit(solution)/shard_map/all_gather | solution.py:765
  9.2 0.7 copy-start.15
  9.9 1.9 copy-start
  10.0 80.7 %all-gather.7.cloned.1.call-start = ((), (), s32[]{:S(2)}) async-start(), calls=%async_computation.5 | async-start | bytes 2875392 | tf_op jit(solution)/shard_map/all_gather | solution.py:764
  10.8 184.5 %all-gather.13.cloned.1.call-start = ((), (), s32[]{:S(2)}) async-start(), calls=%async_computation.8 | async-start | bytes 3833856 | tf_op jit(solution)/shard_map/all_gather | solution.py:766
  11.7 1.1 copy-start.29
  11.7 44.4 %copy-start.23 = (f32[8,64]{1,0:T(8,128)S(1)}, f32[8,64]{1,0:T(8,128)}, u32[]{:S(2)}) copy-start(f32[8,64]{1,0:T(8,128)} %param.33) | copy-start | bytes 6148
  11.7 44.4 %copy-start.22 = (f32[8,40]{1,0:T(8,128)S(1)}, f32[8,40]{1,0:T(8,128)}, u32[]{:S(2)}) copy-start(f32[8,40]{1,0:T(8,128)} %param.32) | copy-start | bytes 3844
  11.7 44.4 %copy-start.17 = (f32[9,416]{1,0:T(8,128)S(1)}, f32[9,416]{1,0:T(8,128)}, u32[]{:S(2)}) copy-start(f32[9,416]{1,0:T(8,128)} %param.31) | copy-start | bytes 44932
  11.7 183.6 %all-gather.11.cloned.1.call-start = ((), (), s32[]{:S(2)}) async-start(), calls=%async_computation.7 | async-start | bytes 5898240 | tf_op jit(solution)/shard_map/all_gather | solution.py:767
  12.7 533.0 %all-reduce.10.cloned.1.call-start = ((), (), s32[]{:S(2)}) async-start(), calls=%async_computation.14 | async-start | bytes 294912 | tf_op jit(solution)/shard_map/psum | solution.py:784
  416.5 10.7 %copy-start.9 = (bf16[1280,320]{1,0:T(8,128)(2,1)S(1)}, bf16[1280,320]{1,0:T(8,128)(2,1)}, u32[]{:S(2)}) copy-start(bf16[1280,320]{1,0:T(8,128)(2,1)} %get-tuple-element.73) | copy-start | bytes 2457604
  416.5 10.7 %copy-start.10 = (bf16[1280,320]{1,0:T(8,128)(2,1)S(1)}, bf16[1280,320]{1,0:T(8,128)(2,1)}, u32[]{:S(2)}) copy-start(bf16[1280,320]{1,0:T(8,128)(2,1)} %get-tuple-element.72) | copy-start | bytes 2457604
  425.8 160.1 %reduce-scatter.8.cloned.1.call-start = ((), (), s32[]{:S(2)}) async-start(), calls=%async_computation.10 | async-start | bytes 921600 | tf_op jit(solution)/shard_map/reduce_scatter | solution.py:775
  426.4 199.5 %reduce-scatter.6.cloned.1.call-start = ((), (), s32[]{:S(2)}) async-start(), calls=%async_computation.9 | async-start | bytes 1105920 | tf_op jit(solution)/shard_map/reduce_scatter | solution.py:775
  427.2 245.5 %reduce-scatter.10.cloned.1.call-start = ((), (), s32[]{:S(2)}) async-start(), calls=%async_computation.11 | async-start | bytes 2875392 | tf_op jit(solution)/shard_map/reduce_scatter | solution.py:775
  430.1 294.0 %reduce-scatter.14.cloned.1.call-start = ((), (), s32[]{:S(2)}) async-start(), calls=%async_computation.13 | async-start | bytes 3833856 | tf_op jit(solution)/shard_map/reduce_scatter | solution.py:775
  430.8 353.0 %reduce-scatter.12.cloned.1.call-start = ((), (), s32[]{:S(2)}) async-start(), calls=%async_computation.12 | async-start | bytes 5898240 | tf_op jit(solution)/shard_map/reduce_scatter | solution.py:775
  549.8 174.3 %copy-start.19 = (f32[8,512]{1,0:T(8,128)}, f32[8,512]{1,0:T(8,128)S(1)}, u32[]{:S(2)}) copy-start(f32[8,512]{1,0:T(8,128)S(1)} %reshape.113) | copy-start | bytes 49156
  902.9 48.6 %copy-start.24 = (f32[8,64]{1,0:T(8,128)S(1)}, f32[8,64]{1,0:T(8,128)}, u32[]{:S(2)}) copy-start(f32[8,64]{1,0:T(8,128)} %param.33) | copy-start | bytes 6148
  902.9 48.6 %copy-start.27 = (f32[8,64]{1,0:T(8,128)S(1)}, f32[8,64]{1,0:T(8,128)}, u32[]{:S(2)}) copy-start(f32[8,64]{1,0:T(8,128)} %param.40) | copy-start | bytes 6148
  902.9 48.6 %copy-start.28 = (f32[8,64]{1,0:T(8,128)S(1)}, f32[8,64]{1,0:T(8,128)}, u32[]{:S(2)}) copy-start(f32[8,64]{1,0:T(8,128)} %param.47) | copy-start | bytes 6148
  952.9 3.5 copy-start.1
  952.9 3.5 copy-start.7
  952.9 3.5 copy-start.8
  956.4 2.6 copy-start.4
  956.4 2.6 copy-start.5
  956.4 2.6 copy-start.11
  956.4 2.6 copy-start.12
  959.0 1.6 copy-start.6
  959.1 1.6 copy-start.13
  959.1 1.6 copy-start.14
  960.7 1.3 copy-start.25
  960.7 1.3 copy-start.26
  960.7 1.9 copy-start.16
  960.7 1.9 copy-start.18
  960.7 1.9 copy-start.20
  960.7 1.9 copy-start.21
Sparse Core Ops, SparseCore 0:
  10.5 29.5 all-gather.8
  42.5 30.3 all-gather.6
  75.4 33.3 all-gather.12
  111.1 41.1 all-gather.10
  426.0 119.7 all-reduce.9
  549.5 36.4 reduce-scatter.7
  590.1 35.7 reduce-scatter.5
  629.3 43.3 reduce-scatter.9
  676.5 47.4 reduce-scatter.13
  727.3 56.5 reduce-scatter.11

commit v2 on v1

--- a/solution.py
+++ b/solution.py
@@ -135,6 +135,64 @@
     if at == 2:
         return moved[image, 1, start : start + 16, :, lanes]
     return plain[image, at, start : start + 16, :, lanes]
+
+
+def up(value, unit):
+    return -(-value // unit) * unit
+
+
+def rows4(shards, groups):
+    return up(10 * (C4 // shards) + (4 * C3 + F4) // shards, 8 * groups)
+
+
+def places3(shards, groups):
+    tall = (PATCH + 4 * C3 + F3) // shards // 2
+    mats = up(tall, 16)
+    slot = up(C3 // shards, 8)
+    flat = up(mats + 4 * slot, 16)
+    flat_rows = -(-(9 * (F3 + F4) + 2 * C3 + 8 * C4) // (shards * 2 * C3))
+    last = flat + up(flat_rows, 8)
+    return mats, slot, flat, flat_rows, last, up(last + 8, 8 * groups)
+
+
+def send_off(out, keep, send, sems, core):
+    def move(at, target):
+        return pltpu.make_async_copy(out.at[at], target.at[at // 2], sems.at[at])
+
+    for at in range(out.shape[0]):
+
+        @pl.when(core == at % 2)
+        def _():
+            move(at, keep).start()
+
+        @pl.when(core != at % 2)
+        def _():
+            move(at, send).start()
+
+    for at in range(out.shape[0]):
+        move(at, keep).wait()
+
+
+def store_columns4(out, value, column):
+    size = C4 // out.shape[0]
+    block, lane = column // C4, column % C4
+    start = block * size
+    lanes = slice(lane, lane + value.shape[1])
+    if not isinstance(column, int):
+        start = pl.multiple_of(start, size)
+        lanes = pl.ds(pl.multiple_of(lane, LC), value.shape[1])
+    for at in range(out.shape[0]):
+        out[at, pl.ds(start, size), lanes] = value[at * size : at * size + size].astype(BF)
+
+
+def store_rows(out, value, row, size, offset):
+    at = row
+    while at < row + value.shape[0]:
+        shard = at // size
+        end = min((shard + 1) * size, row + value.shape[0])
+        start = offset + at - shard * size
+        out[shard, start : start + end - at, :] = value[at - row : end - row].astype(BF)
+        at = end
 
 
 TAPS = [(t, t // 3 - 1, t % 3 - 1) for t in range(9)]
@@ -219,9 +277,9 @@
 
 
 def section4(
-    labels, valid, inv_count, x2, mat4, tall4, depth, norms,
-    dx2_o, gm_o, gt_o, gd_o, gn_o, loss_o,
-    first, y1_s, y2_s, h_s, qkv_s, p_s, mix_s, n_s, hid_s, slope_s, act_s, plain, moved, gd_s,
+    labels, valid, inv_count, core, x2, mat4, tall4, depth, norms,
+    dx2_o, keep, send, gd_o, gn_o, loss_o,
+    out, sems, first, y1_s, y2_s, h_s, qkv_s, p_s, mix_s, n_s, hid_s, slope_s, act_s, plain, moved, gd_s,
 ):
     for ref in (plain, moved):
         for at in (0, 17):
@@ -229,6 +287,9 @@
 
     w1_at = 4 * C4
     wc_at = 4 * C4 + F4
+    shards = out.shape[0]
+    tall_rows = (4 * C3 + F4) // shards
+    tall_at = 10 * (C4 // shards)
 
     for i in range(IMGS):
         rows = pl.ds(i * TOK4, TOK4)
@@ -242,7 +303,9 @@
         h_s[rows, :] = (normalize(y0)[0] * norms[2:3] + norms[3:4]).astype(BF)
     for j in range(3):
         wide = slice(j * C4, j * C4 + C4)
-        qkv_s[:, wide] = nn(h_s[...], mat4[:, wide]).astype(BF)
+        for i in range(IMGS):
+            rows = pl.ds(i * TOK4, TOK4)
+            qkv_s[rows, wide] = nn(h_s[rows, :], mat4[:, wide]).astype(BF)
 
     def attend(i, carry):
         rows = pl.ds(pl.multiple_of(i * TOK4, TOK4), TOK4)
@@ -320,7 +383,11 @@
     loss_o[...] = jnp.broadcast_to(jnp.sum(present[:, 0:1] * ce, axis=0, keepdims=True), (8, 128))
     dlogits = (present * inv_count[0] * (exponent / mass - goal)).astype(BF)
 
-    gm_o[:, wc_at:] = tn(pooled, dlogits).astype(gm_o.dtype)
+    dclass = tn(pooled, dlogits)
+    store_columns4(out, dclass[:, :C4], wc_at)
+    store_columns4(out, jnp.concatenate([dclass[:, C4:], jnp.zeros((C4, 2 * C4 - CLASSES), F32)], axis=1), wc_at + C4)
+    if tall_at + tall_rows < out.shape[1]:
+        out[:, tall_at + tall_rows :, :] = jnp.zeros((shards, out.shape[1] - tall_at - tall_rows, C4), BF)
     dpool = nt(dlogits, mat4[:, wc_at:])
     dgain = None
     for i in range(IMGS):
@@ -335,15 +402,14 @@
     gn_o[7:8] = column_sum(dpool)
 
     dy = y2_s[...].astype(BF)
-    gt_o[4 * C3 :, :] = tn(act_s[...], dy).astype(gt_o.dtype)
+    for at in range(0, F4, 512):
+        store_rows(out, tn(act_s[:, at : at + 512], dy), 4 * C3 + at, tall_rows, tall_at)
     act_s[:, 0:C4] = dy
-    act_s[:, C4 : 2 * C4] = jnp.zeros((IMGS * TOK4, C4), BF)
     gd_s[...] = jnp.zeros_like(gd_s)
     nt_val = n_s[...].T
 
     def feed_back(j, total):
         wide = pl.ds(pl.multiple_of(j * LC, LC), LC)
-        w1_wide = pl.ds(pl.multiple_of(w1_at + j * LC, LC), LC)
         w2 = tall4[pl.ds(pl.multiple_of(4 * C3 + j * LC, LC), LC), :]
         for i in range(IMGS):
             rows = pl.ds(i * TOK4, TOK4)
@@ -358,27 +424,24 @@
                 for qx in range(2):
                     rows = pl.ds(i * TOK4 + qx * 128, 128)
                     base = hid_s[rows, out_lanes].astype(F32).reshape(16, 8, 128)
-                    out = None
+                    acc = None
                     for t, dy, dx in TAPS:
                         value = tap4(plain, moved, i, qx, -dy, -dx, lanes)
                         term = value * kernel[t : t + 1][None]
-                        out = term if out is None else out + term
+                        acc = term if acc is None else acc + term
                         part = jnp.sum(value * base, axis=0)
                         sums[t] = part if sums[t] is None else sums[t] + part
-                    hid_s[rows, out_lanes] = out.reshape(128, 128).astype(BF)
+                    hid_s[rows, out_lanes] = acc.reshape(128, 128).astype(BF)
             for t in range(9):
                 gd_s[t, :, out_lanes] = sums[t]
         dhid = hid_s[:, wide]
-        gm_o[:, w1_wide] = nn(nt_val, dhid).astype(gm_o.dtype)
-        return carry_none
-
-    carry_none = 0
+        store_columns4(out, nn(nt_val, dhid), w1_at + j * LC)
+        return total
+
     lax.fori_loop(0, F4 // LC, feed_back, 0)
     for t in range(9):
         gd_o[t : t + 1, :] = column_sum(gd_s[t])
 
-    for ref_at in (2, 4, 0):
-        pass
     dgain = dshift = None
     for i in range(IMGS):
         rows = pl.ds(i * TOK4, TOK4)
@@ -392,8 +455,10 @@
     gn_o[5:6] = dshift
 
     dprod = y2_s[...].astype(BF)
-    gm_o[:, 3 * C4 : 4 * C4] = nn(mix_s[...], dprod).astype(gm_o.dtype)
-    n_s[...] = nt(dprod, mat4[:, 3 * C4 : 4 * C4]).astype(BF)
+    store_columns4(out, nn(mix_s[...], dprod), 3 * C4)
+    for i in range(IMGS):
+        rows = pl.ds(i * TOK4, TOK4)
+        n_s[rows, :] = nt(dprod[i * TOK4 : i * TOK4 + TOK4], mat4[:, 3 * C4 : 4 * C4]).astype(BF)
 
     def attend_back(i, carry):
         rows = pl.ds(pl.multiple_of(i * TOK4, TOK4), TOK4)
@@ -425,7 +490,7 @@
     ht = h_s[...].T
     for j in range(3):
         wide = slice(j * C4, j * C4 + C4)
-        gm_o[:, wide] = nn(ht, qkv_s[:, wide]).astype(gm_o.dtype)
+        store_columns4(out, nn(ht, qkv_s[:, wide]), j * C4)
 
     sums = [None] * 4
     for i in range(IMGS):
@@ -446,7 +511,8 @@
         for i in range(IMGS):
             part = tn(x2[i, plane * 256 : plane * 256 + 256, :], n_s[i * TOK4 : i * TOK4 + TOK4, :])
             total = part if total is None else total + part
-        gt_o[plane * C3 : plane * C3 + C3, :] = total.astype(gt_o.dtype)
+        store_rows(out, total, plane * C3, tall_rows, tall_at)
+    send_off(out, keep, send, sems, core[0])
 
 
 def feed3_back(dx2, x1, n, hid, slope, act, tall3, mat3, depth, norms, dx1_o, g1_o, g2_o, gd_o, gn_o,
@@ -515,8 +581,8 @@
             gd_o[t : t + 1, :] = column_sum(accd[t])
 
 
-def attend3_back(dx1, z, h, red, q, k, v, p, mix, patches, tall3, mat3, norms, ge_o, gr_o, gm_o, gn_o,
-                 acce, accr, accq, acck, accv, acco, accn, dk_s, dv_s, kt_s, dqt_s, dr_s):
+def attend3_back(groups, core, dx1, z, h, red, q, k, v, p, mix, patches, tall3, mat3, norms, g1, g2, flat, keep, send, out, sems,
+                 tall_s, acce, accr, accq, acck, accv, acco, accn, dk_s, dv_s, kt_s, dqt_s, dr_s):
     step = pl.program_id(0)
 
     @pl.when(step == 0)
@@ -590,13 +656,31 @@
 
     @pl.when(step == IMGS - 1)
     def _():
-        ge_o[...] = acce[...].T.astype(ge_o.dtype)
-        gr_o[...] = accr[...].astype(gr_o.dtype)
-        gm_o[:, 0:C3] = accq[...].T.astype(gm_o.dtype)
-        gm_o[:, C3P : 2 * C3P] = acck[...].astype(gm_o.dtype)
-        gm_o[:, 2 * C3P : 3 * C3P] = accv[...].astype(gm_o.dtype)
-        gm_o[:, 3 * C3P : 3 * C3P + C3] = acco[...].astype(gm_o.dtype)
-        gn_o[...] = accn[...]
+        shards = out.shape[0]
+        mats, slot, flat_at, flat_rows, last, total_rows = places3(shards, groups)
+        mat_rows = C3 // shards
+        tall = (PATCH + 4 * C3 + F3) // shards // 2
+        out[:, mats:, :] = jnp.zeros((shards, total_rows - mats, 2 * C3), BF)
+        if tall < mats:
+            out[:, tall:mats, :] = jnp.zeros((shards, mats - tall, 2 * C3), BF)
+        tall_s[0:PATCH] = acce[...].T
+        tall_s[PATCH : PATCH + 4 * C3] = accr[...]
+        tall_s[PATCH + 4 * C3 :] = g2[...].astype(F32)
+        accq[...] = accq[...].T
+        for at in range(shards):
+            rows = slice(at * mat_rows, at * mat_rows + mat_rows)
+            pieces = [accq[rows, :], acck[rows, 0:C3], accv[rows, 0:C3], acco[rows, :]]
+            start = at * 2 * tall
+            pairs = [tall_s[start : start + tall], tall_s[start + tall : start + 2 * tall]]
+            out[at, 0:tall, :] = jnp.concatenate(pairs, axis=1).astype(BF)
+            for b in range(2):
+                pair = jnp.concatenate(pieces[2 * b : 2 * b + 2], axis=1)
+                out[at, mats + b * slot : mats + b * slot + mat_rows, :] = pair.astype(BF)
+                feed = g1[rows, b * 2 * C3 : b * 2 * C3 + 2 * C3]
+                out[at, mats + (b + 2) * slot : mats + (b + 2) * slot + mat_rows, :] = feed.astype(BF)
+            out[at, flat_at : flat_at + flat_rows, :] = flat[at]
+            out[at, last : last + 6, 0:mat_rows] = accn[:, rows].astype(BF)
+        send_off(out, keep, send, sems, core[0])
 
 
 def whole(shape, dtype=None):
@@ -609,6 +693,10 @@
 
 def sds(*shape, dtype=F32):
     return jax.ShapeDtypeStruct(shape, dtype)
+
+
+def work(microseconds):
+    return pl.CostEstimate(flops=microseconds * 10**9, bytes_accessed=microseconds * 3 * 10**6, transcendentals=0)
 
 
 PARAMS = pltpu.CompilerParams(vmem_limit_bytes=VMEM_BYTES, dimension_semantics=("arbitrary",))
@@ -631,6 +719,7 @@
         scratch_shapes=[pltpu.VMEM((TOK3, C3), F32), pltpu.VMEM((C3P, 256), BF)],
         compiler_params=PARAMS,
         name="embed_attend",
+        cost_estimate=work(58),
     )(patches, tall3, mat3, norms3)
 
 
@@ -647,22 +736,26 @@
         scratch_shapes=[pltpu.VMEM((8, 18, 8, LC), F32), pltpu.VMEM((4, 18, 8, LC), F32)],
         compiler_params=PARAMS,
         name="feed3",
+        cost_estimate=work(47),
     )(x1, tall3, mat3, depth, norms3)
 
 
-def run_section4(labels, valid, inv_count, x2, mat4, tall4, depth, norms4):
+def run_section4(labels, valid, inv_count, core, x2, mat4, tall4, depth, norms4, shards, groups):
     vm = pl.BlockSpec(memory_space=pltpu.VMEM)
     sm = pl.BlockSpec(memory_space=pltpu.SMEM)
+    hbm = pl.BlockSpec(memory_space=pl.ANY)
     rows = IMGS * TOK4
+    half = sds(shards // 2, rows4(shards, groups), C4, dtype=BF)
     return pl.pallas_call(
         section4,
-        in_specs=[sm, sm, sm, vm, vm, vm, vm, vm],
-        out_specs=[vm] * 6,
+        in_specs=[sm, sm, sm, sm, vm, vm, vm, vm, vm],
+        out_specs=[vm, hbm, hbm, vm, vm, vm],
         out_shape=[
-            sds(IMGS, TOK3, C3, dtype=BF), sds(*mat4.shape, dtype=BF), sds(*tall4.shape, dtype=BF), sds(9, F4), sds(8, C4),
+            sds(IMGS, TOK3, C3, dtype=BF), half, half, sds(9, F4), sds(8, C4),
             sds(8, 128),
         ],
         scratch_shapes=[
+            pltpu.VMEM((shards,) + half.shape[1:], BF), pltpu.SemaphoreType.DMA((shards,)),
             pltpu.VMEM((rows, C4), F32), pltpu.VMEM((rows, C4), F32), pltpu.VMEM((rows, C4), F32),
             pltpu.VMEM((rows, C4), BF), pltpu.VMEM((rows, 3 * C4), BF), pltpu.VMEM((IMGS * H4, 256, 256), BF),
             pltpu.VMEM((C4, rows), BF), pltpu.VMEM((rows, C4), BF), pltpu.VMEM((rows, F4), BF),
@@ -671,7 +764,8 @@
         ],
         compiler_params=pltpu.CompilerParams(vmem_limit_bytes=VMEM_BYTES),
         name="section4",
-    )(labels, valid, inv_count, x2, mat4, tall4, depth, norms4)
+        cost_estimate=work(90),
+    )(labels, valid, inv_count, core, x2, mat4, tall4, depth, norms4)
 
 
 def run_feed3_back(dx2, x1, n, hid, slope, act, tall3, mat3, depth, norms3):
@@ -683,7 +777,7 @@
             per_image(TOK3, F3), whole(tall3.shape), whole(mat3.shape), whole(depth.shape), whole(norms3.shape),
         ],
         out_specs=[per_image(TOK3, C3), whole((C3, F3)), whole((F3, C3)), whole((9, F3)), whole((2, C3))],
-        out_shape=[sds(IMGS, TOK3, C3), sds(C3, F3, dtype=BF), sds(F3, C3, dtype=BF), sds(9, F3), sds(2, C3)],
+        out_shape=[sds(IMGS, TOK3, C3), sds(C3, F3), sds(F3, C3, dtype=BF), sds(9, F3), sds(2, C3)],
         scratch_shapes=[
             pltpu.VMEM((C3, F3), F32), pltpu.VMEM((C3, F3), F32), pltpu.VMEM((9, 8, F3), F32), pltpu.VMEM((2, C3), F32),
             pltpu.VMEM((8, 18, 8, LC), F32), pltpu.VMEM((4, 18, 8, LC), F32), pltpu.VMEM((TOK3, C3), BF),
@@ -691,21 +785,28 @@
         ],
         compiler_params=PARAMS,
         name="feed3_back",
+        cost_estimate=work(68),
     )(dx2, x1, n, hid, slope, act, tall3, mat3, depth, norms3)
 
 
-def run_attend3_back(dx1, z, h, red, q, k, v, p, mix, patches, tall3, mat3, norms3):
+def run_attend3_back(core, dx1, z, h, red, q, k, v, p, mix, patches, tall3, mat3, norms3, g1, g2, flat, groups):
+    shards = flat.shape[0]
+    total_rows = places3(shards, groups)[-1]
     return pl.pallas_call(
-        attend3_back,
+        functools.partial(attend3_back, groups),
         grid=(IMGS,),
         in_specs=[
+            pl.BlockSpec(memory_space=pltpu.SMEM),
             per_image(TOK3, C3), per_image(TOK3, C3), per_image(TOK3, C3), per_image(256, C3), per_image(TOK3, C3P),
             per_image(256, C3P), per_image(256, C3P), per_image(H3, 256, TOK3), per_image(C3, TOK3),
             per_image(TOK3, PATCH), whole(tall3.shape), whole(mat3.shape), whole(norms3.shape),
+            whole(g1.shape), whole(g2.shape), whole(flat.shape),
         ],
-        out_specs=[whole((PATCH, C3)), whole((4 * C3, C3)), whole((C3, 4 * C3P)), whole((6, C3))],
-        out_shape=[sds(PATCH, C3, dtype=BF), sds(4 * C3, C3, dtype=BF), sds(C3, 4 * C3P, dtype=BF), sds(6, C3)],
+        out_specs=[pl.BlockSpec(memory_space=pl.ANY)] * 2,
+        out_shape=[sds(shards // 2, total_rows, 2 * C3, dtype=BF)] * 2,
         scratch_shapes=[
+            pltpu.VMEM((shards, total_rows, 2 * C3), BF), pltpu.SemaphoreType.DMA((shards,)),
+            pltpu.VMEM((PATCH + 4 * C3 + F3, C3), F32),
             pltpu.VMEM((C3, PATCH), F32), pltpu.VMEM((4 * C3, C3), F32), pltpu.VMEM((C3, C3), F32),
             pltpu.VMEM((C3, C3P), F32), pltpu.VMEM((C3, C3P), F32), pltpu.VMEM((C3, C3), F32), pltpu.VMEM((6, C3), F32),
             pltpu.VMEM((256, C3P), F32), pltpu.VMEM((256, C3P), F32), pltpu.VMEM((C3P, 256), BF),
@@ -713,7 +814,8 @@
         ],
         compiler_params=PARAMS,
         name="attend3_back",
-    )(dx1, z, h, red, q, k, v, p, mix, patches, tall3, mat3, norms3)
+        cost_estimate=work(65),
+    )(core, dx1, z, h, red, q, k, v, p, mix, patches, tall3, mat3, norms3, g1, g2, flat)
 
 
 def pad_mat3(mat):
@@ -728,13 +830,57 @@
     return grid.transpose(0, 2, 5, 4, 1, 3, 6).reshape(patches.shape)
 
 
-def local_gradients(patches, labels, valid, inv_count, mat3, tall3, mat4, tall4, depth, norms3, norms4):
-    z, h, red, q, k, v, p, mix, x1 = run_embed_attend(patches, tall3, mat3, norms3)
-    n, hid, slope, act, x2 = run_feed3(x1, tall3, mat3, depth[:, :F3], norms3)
-    dx2, gm4, gt4, gd4, gn4, loss = run_section4(labels, valid, inv_count, x2, mat4, tall4, depth[:, F3:], norms4)
-    dx1, g1, g2, gd3, gn3b = run_feed3_back(dx2, x1, n, hid, slope, act, tall3, mat3, depth[:, :F3], norms3)
-    ge, gr, gm3, gn3a = run_attend3_back(dx1, z, h, red, q, k, v, p, mix, patches, tall3, mat3, norms3)
-    return loss, gm4, gt4, gd4, gn4, g1, g2, gd3, gn3b, ge, gr, gm3, gn3a
+def swap(value, axis, mask):
+    return lax.ppermute(value, axis, [(at, at ^ mask) for at in range(lax.axis_size(axis))])
+
+
+def pick(value, index, axis=0):
+    return lax.dynamic_index_in_dim(value, index, axis, keepdims=False)
+
+
+def add_all(own, parts):
+    total = own.astype(F32)
+    for part in parts:
+        total = total + part.astype(F32)
+    return total
+
+
+def chip_sends(keep, got):
+    chip = lax.axis_index("fsdp") // 2
+    sums = [add_all(pick(keep, chip ^ mask), [pick(got, chip ^ mask)]) for mask in range(keep.shape[0])]
+    return sums[0], [one.astype(BF) for one in sums[1:]]
+
+
+def depth_sends(shard):
+    count, me = lax.axis_size("dp"), lax.axis_index("dp")
+    cut = shard.reshape(count, shard.shape[0] // count, shard.shape[1])
+    return pick(cut, me), [pick(cut, me ^ mask).astype(BF) for mask in range(1, count)]
+
+
+def exchange(sends, axis, unit):
+    return [swap(send, axis, unit * (at + 1)) for at, send in enumerate(sends)]
+
+
+def depth_gather(piece):
+    count, me = lax.axis_size("dp"), lax.axis_index("dp")
+    narrow = piece.astype(BF)
+    parts = [narrow] + [swap(narrow, "dp", mask) for mask in range(1, count)]
+    placed = [lax.select_n(me, *[parts[at ^ other] for other in range(count)]) for at in range(count)]
+    return jnp.concatenate(placed, axis=0).astype(F32)
+
+
+def total_over(axis, value):
+    mask = 1
+    while mask < lax.axis_size(axis):
+        value = value + swap(value, axis, mask)
+        mask *= 2
+    return value
+
+
+def total_over_all(row):
+    count = lax.axis_size("dp") * lax.axis_size("fsdp")
+    rows = jnp.broadcast_to(row, (count, row.shape[1]))
+    return jnp.sum(lax.all_to_all(rows, ("dp", "fsdp"), 0, 0, tiled=True), axis=0, keepdims=True)
 
 
 def adamw(master, moment, second, gradient, is_norm):
@@ -750,69 +896,100 @@
 
 def body(patches, labels, valid, *state):
     masters, moments, seconds = state[0:7], state[7:14], state[14:21]
-    both = ("dp", "fsdp")
-    image_count = lax.psum(jnp.sum(valid).astype(F32), both)
-    inv_count = (1.0 / image_count).reshape(1)
-
+    shards, groups = lax.axis_size("fsdp"), lax.axis_size("dp")
     mat3, tall3, mat4, tall4, depth, norms3, norms4 = [master.astype(BF) for master in masters]
+    half, m_rows = tall3.shape[0] // 2, mat3.shape[0]
+    pack = [jnp.concatenate([tall3[:half], tall3[half:]], axis=1)]
+    pack += [mat3[:, at * 2 * C3 : at * 2 * C3 + 2 * C3] for at in range(4)]
+    pack = lax.all_gather(jnp.concatenate(pack, axis=0), "fsdp", axis=0)
+
     small = [jnp.pad(piece.T, ((0, 0), (0, 16 - piece.shape[0]))) for piece in (depth, norms3, norms4)]
+    small.append(jnp.full((8, 16), jnp.sum(valid)).astype(BF))
     sizes = [piece.shape[0] for piece in small]
     small = lax.all_gather(jnp.concatenate(small, axis=0), "fsdp", axis=0)
-    edges = [0, sizes[0], sizes[0] + sizes[1], sum(sizes)]
+    edges = [0, sizes[0], sizes[0] + sizes[1], sum(sizes[:3])]
     parts = [small[:, edges[at] : edges[at + 1]].reshape(-1, 16).T.astype(F32) for at in range(3)]
     depth_all, norms3_all, norms4_all = parts[0][:9], parts[1][:8], parts[2][:8]
-    tall3_all = lax.all_gather(tall3, "fsdp", axis=0, tiled=True)
-    mat3_all = lax.all_gather(pad_mat3(mat3), "fsdp", axis=0, tiled=True)
+    present = jnp.full((8, 128), jnp.sum(small[:, edges[3], 0].astype(F32)))
+    image_count = total_over("dp", present)[0, 0]
+    inv_count = (1.0 / image_count).reshape(1)
+
+    tall3_all = jnp.concatenate([pack[:, :half, :C3], pack[:, :half, C3:]], axis=1).reshape(-1, C3)
+    mats = pack[:, half:].reshape(shards, 4, m_rows, 2 * C3).transpose(1, 0, 2, 3).reshape(4, C3, 2 * C3)
+    mat3_all = [mats[at // 2, :, at % 2 * C3 : at % 2 * C3 + C3] for at in range(4)]
+    mat3_all = [jnp.pad(piece, ((0, 0), (0, C3P - C3))) for piece in mat3_all]
+    mat3_all = jnp.concatenate(mat3_all + [mats[2], mats[3]], axis=1)
     tall4_all = lax.all_gather(tall4, "fsdp", axis=0, tiled=True)
     mat4_all = lax.all_gather(mat4, "fsdp", axis=0, tiled=True)
 
-    loss, gm4, gt4, gd4, gn4, g1, g2, gd3, gn3b, ge, gr, gm3, gn3a = local_gradients(
-        reorder(patches.reshape(IMGS, TOK3, PATCH)), labels.reshape(IMGS), valid.reshape(IMGS), inv_count,
-        mat3_all, tall3_all, mat4_all, tall4_all, depth_all, norms3_all, norms4_all,
+    patches = reorder(patches.reshape(IMGS, TOK3, PATCH))
+    depth3, depth4 = depth_all[:, :F3], depth_all[:, F3:]
+    z, h, red, q, k, v, p, mix, x1 = run_embed_attend(patches, tall3_all, mat3_all, norms3_all)
+    n, hid, slope, act, x2 = run_feed3(x1, tall3_all, mat3_all, depth3, norms3_all)
+    core = (lax.axis_index("fsdp") % 2).reshape(1)
+    dx2, keep4, send4, gd4, gn4, loss = run_section4(
+        labels.reshape(IMGS), valid.reshape(IMGS), inv_count, core, x2, mat4_all, tall4_all, depth4, norms4_all,
+        shards, groups,
     )
 
-    def share(piece):
-        return lax.psum(lax.psum_scatter(piece, "fsdp", scatter_dimension=0, tiled=True).astype(F32), "dp")
-
-    grad_mat4 = share(gm4)
-    grad_tall4 = share(gt4)
-    grad_feed = share(g1)
-    grad_mix = share(gm3)
-    grad_tall3 = share(jnp.concatenate([ge, gr, g2], axis=0))
-    grad_mat3 = jnp.concatenate([grad_mix[:, at * C3P : at * C3P + C3] for at in range(4)] + [grad_feed], axis=1)
-    flat = [gd3.reshape(-1), gd4.reshape(-1), gn3a.reshape(-1), gn3b.reshape(-1), gn4.reshape(-1)]
-    flat = lax.psum(jnp.concatenate(flat), both)
-    me = lax.axis_index("fsdp")
-    ends = [0]
-    for size in (9 * F3, 9 * F4, 6 * C3, 2 * C3, 8 * C4):
-        ends.append(ends[-1] + size)
-    cut = [flat[ends[at] : ends[at + 1]] for at in range(5)]
-    full = [
-        jnp.concatenate([cut[0].reshape(9, F3), cut[1].reshape(9, F4)], axis=1),
-        jnp.concatenate([cut[2].reshape(6, C3), cut[3].reshape(2, C3)], axis=0),
-        cut[4].reshape(8, C4),
-    ]
-    own = [
-        lax.dynamic_slice_in_dim(piece, me * master.shape[1], master.shape[1], 1)
-        for piece, master in zip(full, masters[4:])
-    ]
-    group = [grad_mat3, grad_tall3, grad_mat4, grad_tall4] + own
-
-    square = jnp.float32(0.0)
-    for shard in group:
-        square = square + jnp.sum(shard * shard)
-    dp_count = lax.axis_size("dp")
-    totals = lax.psum(jnp.stack([square / dp_count, loss[0, 0]]), both)
-    grad_norm = jnp.sqrt(totals[0])
+    own4, sends4 = chip_sends(keep4, swap(send4, "fsdp", 1))
+    dx2, own4, sends4 = lax.optimization_barrier((dx2, own4, sends4))
+    got4 = exchange(sends4, "fsdp", 2)
+    dx1, g1, g2, gd3, gn3b = run_feed3_back(dx2, x1, n, hid, slope, act, tall3_all, mat3_all, depth3, norms3_all)
+    dx1, own4, got4 = lax.optimization_barrier((dx1, own4, got4))
+    own4, sends4 = depth_sends(add_all(own4, got4))
+
+    def by_columns(grad):
+        return grad.reshape(grad.shape[0], shards, -1).transpose(1, 0, 2).reshape(shards, -1)
+
+    _, slot, flat_at, flat_rows, last, _ = places3(shards, groups)
+    flat = jnp.concatenate([by_columns(grad) for grad in (jnp.concatenate([gd3, gd4], axis=1), gn3b, gn4)], axis=1)
+    flat = jnp.pad(flat, ((0, 0), (0, flat_rows * 2 * C3 - flat.shape[1])))
+    flat = flat.reshape(shards, flat_rows, 2 * C3).astype(BF)
+    dx1, own4, sends4, flat = lax.optimization_barrier((dx1, own4, sends4, flat))
+    got4 = exchange(sends4, "dp", 1)
+    keep3, send3 = run_attend3_back(
+        core, dx1, z, h, red, q, k, v, p, mix, patches, tall3_all, mat3_all, norms3_all, g1, g2, flat, groups
+    )
+    keep3, send3, got4 = lax.optimization_barrier((keep3, send3, got4))
+    piece4 = add_all(own4, got4)
+    own3, sends3 = chip_sends(keep3, swap(send3, "fsdp", 1))
+    own3, sends3, piece4 = lax.optimization_barrier((own3, sends3, piece4))
+    got3 = exchange(sends3, "fsdp", 2)
+    grads4 = depth_gather(piece4)
+    own3, got3, grads4 = lax.optimization_barrier((own3, got3, grads4))
+    own3, sends3 = depth_sends(add_all(own3, got3))
+    piece3 = add_all(own3, exchange(sends3, "dp", 1))
+    square = jnp.sum(piece4 * piece4) + jnp.sum(piece3 * piece3)
+    lane = lax.broadcasted_iota(jnp.int32, (1, 128), 1)
+    totals = total_over_all(jnp.where(lane == 0, square, loss[0:1]))
+    grads3 = depth_gather(piece3)
+
+    m_rows, t_rows = C4 // shards, masters[3].shape[0]
+    blocks4 = [grads4[at * m_rows : at * m_rows + m_rows] for at in range(10)]
+    grad_mat4 = jnp.concatenate(blocks4, axis=1)[:, : masters[2].shape[1]]
+    grad_tall4 = grads4[10 * m_rows : 10 * m_rows + t_rows]
+    t_rows, m_rows = masters[1].shape[0], masters[0].shape[0]
+    mats_at, half = up(t_rows // 2, 16), t_rows // 2
+    grad_tall3 = jnp.concatenate([grads3[:half, :C3], grads3[:half, C3:]], axis=0)
+    grad_mat3 = jnp.concatenate([grads3[mats_at + at * slot : mats_at + at * slot + m_rows] for at in range(4)], axis=1)
+    flat = grads3[flat_at : flat_at + flat_rows].reshape(-1)
+    sizes = [9 * t_rows, 2 * m_rows, masters[6].size]
+    grad_depth = flat[: sizes[0]].reshape(9, t_rows)
+    grad_norms3 = jnp.concatenate(
+        [grads3[last : last + 6, :m_rows], flat[sizes[0] : sizes[0] + sizes[1]].reshape(2, m_rows)], axis=0
+    )
+    grad_norms4 = flat[sizes[0] + sizes[1] : sum(sizes)].reshape(masters[6].shape)
+    group = [grad_mat3, grad_tall3, grad_mat4, grad_tall4, grad_depth, grad_norms3, grad_norms4]
+
+    grad_norm = jnp.sqrt(totals[0, 0])
     clip_factor = jnp.minimum(1.0, CLIP_LEVEL / (grad_norm + 1e-06))
-    results = [
-        adamw(masters[at], moments[at], seconds[at], clip_factor * group[at], at >= 5) for at in range(7)
-    ]
+    results = [adamw(masters[at], moments[at], seconds[at], clip_factor * group[at], at >= 5) for at in range(7)]
     return (
         *[result[0] for result in results],
         *[result[1] for result in results],
         *[result[2] for result in results],
-        totals[1],
+        totals[0, 1],
         image_count,
         grad_norm,
     )

time: 976 us -> 524 us (0.54)
  waiting for transfers between devices: 347 us -> 32.2 us
  blocking collectives: 207 us -> 10.7 us
  starting transfers between devices: 0.4 us -> 32.7 us
  other arithmetic: 28.3 us -> 46.7 us
    reduce_scatter x5 -> x0, waiting for transfers between devices: 231 us -> none  [share(): lax.psum_scatter(piece, 'fsdp', scatter_dimension=0, tiled=True).astype(F32)]
    psum x3 -> x0, blocking collectives: 197 us -> none  [the longest x1 117 us: share(): lax.psum(lax.psum_scatter(piece, 'fsdp', scatter_dimension=0, tiled=True)...]
    psum x1 -> x0, waiting for transfers between devices: 113 us -> none  [body(): flat = lax.psum(jnp.concatenate(flat), both)]
    ppermute x0 -> x22, waiting for transfers between devices: none -> 30 us  [swap(): lax.ppermute(value, axis, [(at, at ^ mask) for at in range(lax.axis_size(...]
    ppermute x0 -> x22, starting transfers between devices: none -> 28.8 us  [swap(): lax.ppermute(value, axis, [(at, at ^ mask) for at in range(lax.axis_size(...]
    convert_element_type x0 -> x4, other arithmetic: none -> 10.1 us  [the longest x2 9.76 us: chip_sends(): return (sums[0], [one.astype(BF) for one in sums[1:]])]
  transfers between devices with their start and end apart: 10 -> 26, of which waited for: 6 -> 8; matrix products, arithmetic and copies ran while one was open for 4% -> 10% of each run, Pallas kernels for 11% -> 46%
where the time goes in v2:
time: 524 us; the launch traced here: 514 us
  Pallas kernels  329 us (63%)
  other arithmetic  46.7 us (9%)
  local copies, waits for them, and re-layouts  43.1 us (8%)
  starting transfers between devices  32.7 us (6%)
  waiting for transfers between devices  32.2 us (6%)
  between operations  19.6 us (4%)
  blocking collectives  10.7 us (2%)
    pallas_call x1, Pallas kernels, run_section4(): pl.pallas_call(section4, in_specs=[sm, sm, sm, sm, vm, vm, vm, vm, vm], o...  91.3 us
    pallas_call x1, Pallas kernels, run_feed3_back(): pl.pallas_call(feed3_back, grid=(IMGS,), in_specs=[per_image(TOK3, C3), p...  68.7 us
    pallas_call x1, Pallas kernels, run_attend3_back(): pl.pallas_call(functools.partial(attend3_back, groups), grid=(IMGS,), in_...  64.7 us
    pallas_call x1, Pallas kernels, run_embed_attend(): pl.pallas_call(embed_attend, grid=(IMGS,), in_specs=[per_image(TOK3, PATC...  57.9 us
    pallas_call x1, Pallas kernels, run_feed3(): pl.pallas_call(feed3, grid=(IMGS,), in_specs=[per_image(TOK3, C3), whole(...  46.8 us
    ppermute x22, waiting for transfers between devices, swap(): lax.ppermute(value, axis, [(at, at ^ mask) for at in range(lax.axis_size(...  30 us
    ppermute x22, starting transfers between devices, swap(): lax.ppermute(value, axis, [(at, at ^ mask) for at in range(lax.axis_size(...  28.8 us
    another operation x2, local copies, waits for them, and re-layouts, reorder(): grid = patches.reshape(count, 16, 2, 8, 2, 2, patches.shape[-1])  19.8 us
  transfers between devices with their start and end apart: 26, of which 8 were waited for; matrix products, arithmetic and copies ran while one was open for 10% of the time, Pallas kernels for 46%

profile of v2, /device:TPU:0, one launch (start us, length us, event | category | flops | bytes accessed | tf_op | source)
XLA Modules:
  0.0 514.4 jit_solution(10000987415636946745)
XLA Ops:
  7.2 1.0 convert_element_type.259
  8.3 1.2 convert_element_type.258
  9.8 0.8 copy-done.7
  10.6 0.8 convert_element_type.266
  13.0 10.7 %all-gather.2 = bf16[8,528,16]{1,2,0:T(8,128)(2,1)S(1)} all-gather(bf16[1,528,16]{1,2,0:T(8,128)(2,1)S(1)} %fusion.26), channel_id=2, replica_groups=mesh['dp'=4,'fsdp'=8] {'fsdp'}, dimensions={0}, use_global_device_ids=true | all-gather | bytes 152064 | tf_op jit(solution)/shard_map/all_gather | solution.py:909
  25.1 1.6 collective-permute-start
  26.7 0.9 convert_element_type.265
  29.4 2.7 collective-permute-start.1
  34.3 13.3 %reshape_reshape.3 = bf16[4,16,2,8,2,2,768]{6,5,4,3,2,1,0:T(2,128)(2,1)} reshape(bf16[4,1,1024,768]{3,2,1,0:T(8,128)(2,1)} %param.24) | data formatting | bytes 12582912 | tf_op jit(solution)/shard_map/reshape;reshape | solution.py:829
  47.6 6.5 %copy.82 = bf16[4,16,2,8,2,2,768]{6,3,1,4,5,2,0:T(8,128)(2,1)} copy(bf16[4,16,2,8,2,2,768]{6,5,4,3,2,1,0:T(2,128)(2,1)} %reshape_reshape.3) | data formatting | bytes 12582912 | tf_op jit(solution)/shard_map/reshape;reshape | solution.py:829
  56.0 1.6 slice.220
  57.9 2.0 copy-done.2
  59.9 0.7 fusion.40
  61.2 1.2 copy-done.20
  62.4 1.7 pad_maximum_fusion
  64.1 57.9 %embed_attend.1 = (f32[4,1024,320]{2,1,0:T(8,128)}, bf16[4,1024,320]{2,1,0:T(8,128)(2,1)}, f32[4,256,320]{2,1,0:T(8,128)}, bf16[4,1024,384]{2,1,0:T(8,128)(2,1)}...) custom-call(bf16[4,1024,768]{2,1,0:T(8,128)(2,1)} %bitcast.99, ...), custom_call_target="tpu_custom_call" | custom-call | flops 57999998976 | bytes 174000000 | tf_op jit(solution)/shard_map/embed_attend/pallas_call | solution.py:706
  122.0 46.8 %feed3.1 = (bf16[4,1024,320]{2,1,0:T(8,128)(2,1)}, bf16[4,1024,1280]{2,1,0:T(8,128)(2,1)}, bf16[4,1024,1280]{2,1,0:T(8,128)(2,1)}, bf16[4,1024,1280]{2,1,0:T(8,128)(2,1)}, bf16[4,1024,320]{2,1,0:T(8,128)(2,1)}) custom-call(f32[4,1024,320]{2,1,0:T(8,128)} %get-tuple-element.82.x1, bf16[3328,320]{1,0:T(8,128)(2,1)} %bitcast.109, bf16[320,2816]{1,0:T(8,128)(2,1)} %copy-done.20, ...), custom_call_target="tpu_custom_call" | custom-call | flops 46999998464 | bytes 141000000 | tf_op jit(solution)/shard_map/feed3/pallas_call | solution.py:727
  168.9 91.3 %section4.1 = (bf16[4,1024,320]{2,1,0:T(8,128)(2,1)}, bf16[4,1056,512]{2,1,0:T(8,128)(2,1)}, bf16[4,1056,512]{2,1,0:T(8,128)(2,1)}, f32[9,2048]{1,0:T(8,128)}, f32[8,512]{1,0:T(8,128)}, /*index=5*/f32[8,128]{1,0:T(8,128)}) custom-call(s32[4]{0:T(128)} %bitcast.124, s32[4]{0:T(128)} %bitcast.125, f32[1]{0:T(128)} %bitcast.8.inv_count, s32[1]{0:T(128)} %bitcast.core, ...), custom_call_target="tpu_custom_call" | custom-call | flops 89999998976 | bytes 270000000 | tf_op jit(solution)/shard_map/section4/pallas_call | solution.py:749
  260.3 0.9 convert.33
  261.3 0.7 convert.35
  262.2 5.8 %collective-permute-done.2 = bf16[4,1056,512]{2,1,0:T(8,128)(2,1)} collective-permute-done((bf16[4,1056,512]{2,1,0:T(8,128)(2,1)}, bf16[4,1056,512]{2,1,0:T(8,128)(2,1)}, u32[]{:S(2)}, u32[]{:S(2)}) %collective-permute-start.2) | collective-permute-done | bytes 4325408 | tf_op jit(solution)/shard_map/ppermute | solution.py:834
  268.0 6.8 %fusion.3 = (bf16[1056,512]{1,0:T(8,128)(2,1)}, bf16[1056,512]{1,0:T(8,128)(2,1)}, bf16[1056,512]{1,0:T(8,128)(2,1)}, f32[1056,512]{1,0:T(8,128)}) fusion(bf16[4,1056,512]{2,1,0:T(8,128)(2,1)} %collective-permute-done.2, s32[]{:T(128)S(6)} %select_n.205, bf16[4,1056,512]{2,1,0:T(8,128)(2,1)} %get-tuple-element.85, s32[]{:T(128)S(6)} %select_n.204, ...), kind=kLoop, calls=%fused_computation.14 | loop fusion | flops 8110080 | bytes 14057488 | tf_op jit(solution)/shard_map/convert_element_type | solution.py:851
  274.8 1.7 collective-permute-start.3
  276.7 1.6 collective-permute-start.5
  278.3 68.7 %feed3_back.1 = (f32[4,1024,320]{2,1,0:T(8,128)}, f32[320,1280]{1,0:T(8,128)}, bf16[1280,320]{1,0:T(8,128)(2,1)}, f32[9,1280]{1,0:T(8,128)}, f32[2,320]{1,0:T(2,128)}) custom-call(bf16[4,1024,320]{2,1,0:T(8,128)(2,1)} %get-tuple-element.87.dx2, f32[4,1024,320]{2,1,0:T(8,128)} %get-tuple-element.82.x1, bf16[4,1024,320]{2,1,0:T(8,128)(2,1)} %get-tuple-element.88.n, ...), custom_call_target="tpu_custom_call" | custom-call | flops 67999997952 | bytes 204000000 | tf_op jit(solution)/shard_map/feed3_back/pallas_call | solution.py:772
  347.0 0.9 convert.32
  348.2 0.7 convert.34
  349.2 3.1 convert_add_fusion
  352.4 0.9 fusion.12
  353.9 1.7 collective-permute-start.6
  355.7 2.6 collective-permute-start.8
  358.3 64.7 %attend3_back.1 = (bf16[4,384,640]{2,1,0:T(8,128)(2,1)}, bf16[4,384,640]{2,1,0:T(8,128)(2,1)}) custom-call(s32[1]{0:T(128)} %bitcast.core, f32[4,1024,320]{2,1,0:T(8,128)} %get-tuple-element.106.dx1, f32[4,1024,320]{2,1,0:T(8,128)} %get-tuple-element.107.z, bf16[4,1024,320]{2,1,0:T(8,128)(2,1)} %get-tuple-element.108.h, ...), custom_call_target="tpu_custom_call" | custom-call | flops 65000001536 | bytes 195000000 | tf_op jit(solution)/shard_map/attend3_back/pallas_call | solution.py:795
  423.2 1.3 convert_add_fusion.2
  424.4 2.9 collective-permute-done.9
  427.4 2.9 fusion.8
  430.3 0.7 multiply_reduce_fusion
  431.0 0.8 collective-permute-start.13
  431.8 1.0 collective-permute-start.14
  432.8 2.6 collective-permute-start.15
  435.4 1.7 collective-permute-start.10
  437.3 6.3 %collective-permute-done.13 = bf16[264,512]{1,0:T(8,128)(2,1)S(1)} collective-permute-done((bf16[264,512]{1,0:T(8,128)(2,1)S(1)}, bf16[264,512]{1,0:T(8,128)(2,1)S(1)}, u32[]{:S(2)}, u32[]{:S(2)}) %collective-permute-start.13) | collective-permute-done | bytes 270368 | tf_op jit(solution)/shard_map/ppermute | solution.py:834
  443.6 1.4 collective-permute-start.12
  445.0 8.6 %collective-permute-done.14 = bf16[264,512]{1,0:T(8,128)(2,1)S(1)} collective-permute-done((bf16[264,512]{1,0:T(8,128)(2,1)S(1)}, bf16[264,512]{1,0:T(8,128)(2,1)S(1)}, u32[]{:S(2)}, u32[]{:S(2)}) %collective-permute-start.14) | collective-permute-done | bytes 270368 | tf_op jit(solution)/shard_map/ppermute | solution.py:834
  454.1 5.9 %collective-permute-done.11 = bf16[384,640]{1,0:T(8,128)(2,1)S(1)} collective-permute-done((bf16[384,640]{1,0:T(8,128)(2,1)}, bf16[384,640]{1,0:T(8,128)(2,1)S(1)}, u32[]{:S(2)}, u32[]{:S(2)}) %collective-permute-start.11) | collective-permute-done | bytes 491552 | tf_op jit(solution)/shard_map/ppermute | solution.py:834
  460.3 2.0 collective-permute-start.17
  462.3 2.4 collective-permute-start.18
  469.4 0.7 slice_dynamic-update-slice_fusion.2
  471.2 1.3 multiply_reduce_fusion.1
  473.8 0.7 fusion.32
  475.1 3.8 all-to-all-start
  479.6 1.9 collective-permute-start.19
  481.5 2.4 collective-permute-start.20
  484.0 2.1 all-to-all-done
  487.4 4.8 multiply_subtract_fusion
  492.3 1.9 multiply_subtract_fusion.1
  494.2 1.1 select_select_fusion.7
  496.7 0.7 maximum_convert_fusion.5
  497.5 0.8 mul.384
  498.2 0.7 reshape.198
  499.2 1.3 multiply_subtract_fusion.5
  500.5 1.4 multiply_subtract_fusion.4
  501.9 1.3 multiply_subtract_fusion.6
  503.4 1.6 multiply_subtract_fusion.2
  505.0 1.2 multiply_subtract_fusion.3
  (161 shorter events, 21.0 us)
Async XLA Ops:
  7.2 48.8 %all-gather.11.cloned.1.call-start = ((), (), s32[]{:S(2)}) async-start(), calls=%async_computation.3 | async-start | bytes 4239360 | tf_op jit(solution)/shard_map/all_gather | solution.py:904
  8.3 2.4 copy-start.3
  9.5 2.0 copy-start.25
  9.5 3.4 copy-start.21
  9.5 3.4 copy-start.23
  9.6 3.4 copy-start.18
  9.6 17.1 %copy-start = (f32[64,5096]{1,0:T(8,128)S(1)}, f32[64,5096]{1,0:T(8,128)}, u32[]{:S(2)}) copy-start(f32[64,5096]{1,0:T(8,128)} %param.29) | copy-start | bytes 3913732
  9.8 0.8 copy-start.7
  10.6 158.3 %all-gather.9.cloned.1.call-start = ((), (), s32[]{:S(2)}) async-start(), calls=%async_computation.2 | async-start | bytes 3833856 | tf_op jit(solution)/shard_map/all_gather | solution.py:922
  11.5 157.4 %all-gather.7.cloned.1.call-start = ((), (), s32[]{:S(2)}) async-start(), calls=%async_computation.1 | async-start | bytes 5898240 | tf_op jit(solution)/shard_map/all_gather | solution.py:923
  25.1 3.7 collective-permute-start
  29.4 24.7 %collective-permute-start.1 = (f32[8,128]{1,0:T(8,128)S(1)}, f32[8,128]{1,0:T(8,128)S(1)}, u32[]{:S(2)}, u32[]{:S(2)}) collective-permute-start(f32[8,128]{1,0:T(8,128)S(1)} %broadcast_add_fusion), channel_id=1, source_target_pairs={{0,16},{8,24},{16,0},{24,8},{1,17},{9,25},{17,1},{25,9},{2,18},{10... | collective-permute-start | bytes 12296 | tf_op jit(solution)/shard_map/ppermute | solution.py:834
  57.6 2.3 copy-start.2
  61.2 1.2 copy-start.20
  260.2 7.8 %collective-permute-start.2 = (bf16[4,1056,512]{2,1,0:T(8,128)(2,1)}, bf16[4,1056,512]{2,1,0:T(8,128)(2,1)}, u32[]{:S(2)}, u32[]{:S(2)}) collective-permute-start(bf16[4,1056,512]{2,1,0:T(8,128)(2,1)} %get-tuple-element.86), channel_id=1, source_target_pairs={{0,1},{1,0},{2,3},{3,2},{4,5},{5,4},{6,7},{7,6},{8,9},{9,8},{10,11... | collective-permute-start | bytes 12976136 | tf_op jit(solution)/shard_map/ppermute | solution.py:834
  274.8 74.4 %collective-permute-start.3 = (bf16[1056,512]{1,0:T(8,128)(2,1)}, bf16[1056,512]{1,0:T(8,128)(2,1)}, u32[]{:S(2)}, u32[]{:S(2)}) collective-permute-start(bf16[1056,512]{1,0:T(8,128)(2,1)} %get-tuple-element.94), channel_id=1, source_target_pairs={{0,2},{1,3},{2,0},{3,1},{4,6},{5,7},{6,4},{7,5},{8,10},{9,11},{10,... | collective-permute-start | bytes 3244040 | tf_op jit(solution)/shard_map/ppermute | solution.py:834
  276.5 72.7 %collective-permute-start.4 = (bf16[1056,512]{1,0:T(8,128)(2,1)}, bf16[1056,512]{1,0:T(8,128)(2,1)}, u32[]{:S(2)}, u32[]{:S(2)}) collective-permute-start(bf16[1056,512]{1,0:T(8,128)(2,1)} %get-tuple-element.95), channel_id=1, source_target_pairs={{0,4},{1,5},{2,6},{3,7},{4,0},{5,1},{6,2},{7,3},{8,12},{9,13},{10,... | collective-permute-start | bytes 3244040 | tf_op jit(solution)/shard_map/ppermute | solution.py:834
  276.7 72.5 %collective-permute-start.5 = (bf16[1056,512]{1,0:T(8,128)(2,1)}, bf16[1056,512]{1,0:T(8,128)(2,1)}, u32[]{:S(2)}, u32[]{:S(2)}) collective-permute-start(bf16[1056,512]{1,0:T(8,128)(2,1)} %get-tuple-element.96), channel_id=1, source_target_pairs={{0,6},{1,7},{2,4},{3,5},{4,2},{5,3},{6,0},{7,1},{8,14},{9,15},{10,... | collective-permute-start | bytes 3244040 | tf_op jit(solution)/shard_map/ppermute | solution.py:834
  353.9 69.1 %collective-permute-start.6 = (bf16[264,512]{1,0:T(8,128)(2,1)}, bf16[264,512]{1,0:T(8,128)(2,1)}, u32[]{:S(2)}, u32[]{:S(2)}) collective-permute-start(bf16[264,512]{1,0:T(8,128)(2,1)} %get-tuple-element.120), channel_id=1, source_target_pairs={{0,8},{8,0},{16,24},{24,16},{1,9},{9,1},{17,25},{25,17},{2,10},{10... | collective-permute-start | bytes 811016 | tf_op jit(solution)/shard_map/ppermute | solution.py:834
  355.6 67.5 %collective-permute-start.7 = (bf16[264,512]{1,0:T(8,128)(2,1)}, bf16[264,512]{1,0:T(8,128)(2,1)}, u32[]{:S(2)}, u32[]{:S(2)}) collective-permute-start(bf16[264,512]{1,0:T(8,128)(2,1)} %get-tuple-element.121), channel_id=1, source_target_pairs={{0,16},{8,24},{16,0},{24,8},{1,17},{9,25},{17,1},{25,9},{2,18},{10... | collective-permute-start | bytes 811016 | tf_op jit(solution)/shard_map/ppermute | solution.py:834
  355.7 67.4 %collective-permute-start.8 = (bf16[264,512]{1,0:T(8,128)(2,1)S(1)}, bf16[264,512]{1,0:T(8,128)(2,1)}, u32[]{:S(2)}, u32[]{:S(2)}) collective-permute-start(bf16[264,512]{1,0:T(8,128)(2,1)S(1)} %get-tuple-element.122), channel_id=1, source_target_pairs={{0,24},{8,16},{16,8},{24,0},{1,25},{9,17},{17,9},{25,1},{2,26},{10... | collective-permute-start | bytes 811016 | tf_op jit(solution)/shard_map/ppermute | solution.py:834
  423.1 4.2 collective-permute-start.9
  431.0 12.6 %collective-permute-start.13 = (bf16[264,512]{1,0:T(8,128)(2,1)S(1)}, bf16[264,512]{1,0:T(8,128)(2,1)S(1)}, u32[]{:S(2)}, u32[]{:S(2)}) collective-permute-start(bf16[264,512]{1,0:T(8,128)(2,1)S(1)} %get-tuple-element.192), channel_id=1, source_target_pairs={{0,8},{8,0},{16,24},{24,16},{1,9},{9,1},{17,25},{25,17},{2,10},{10... | collective-permute-start | bytes 811016 | tf_op jit(solution)/shard_map/ppermute | solution.py:834
  431.8 21.8 %collective-permute-start.14 = (bf16[264,512]{1,0:T(8,128)(2,1)S(1)}, bf16[264,512]{1,0:T(8,128)(2,1)S(1)}, u32[]{:S(2)}, u32[]{:S(2)}) collective-permute-start(bf16[264,512]{1,0:T(8,128)(2,1)S(1)} %get-tuple-element.192), channel_id=1, source_target_pairs={{0,16},{8,24},{16,0},{24,8},{1,17},{9,25},{17,1},{25,9},{2,18},{10... | collective-permute-start | bytes 811016 | tf_op jit(solution)/shard_map/ppermute | solution.py:834
  432.8 20.9 %collective-permute-start.15 = (bf16[264,512]{1,0:T(8,128)(2,1)S(1)}, bf16[264,512]{1,0:T(8,128)(2,1)S(1)}, u32[]{:S(2)}, u32[]{:S(2)}) collective-permute-start(bf16[264,512]{1,0:T(8,128)(2,1)S(1)} %get-tuple-element.192), channel_id=1, source_target_pairs={{0,24},{8,16},{16,8},{24,0},{1,25},{9,17},{17,9},{25,1},{2,26},{10... | collective-permute-start | bytes 811016 | tf_op jit(solution)/shard_map/ppermute | solution.py:834
  435.4 18.7 %collective-permute-start.10 = (bf16[384,640]{1,0:T(8,128)(2,1)}, bf16[384,640]{1,0:T(8,128)(2,1)S(1)}, u32[]{:S(2)}, u32[]{:S(2)}) collective-permute-start(bf16[384,640]{1,0:T(8,128)(2,1)} %get-tuple-element.131), channel_id=1, source_target_pairs={{0,2},{1,3},{2,0},{3,1},{4,6},{5,7},{6,4},{7,5},{8,10},{9,11},{10,... | collective-permute-start | bytes 1474568 | tf_op jit(solution)/shard_map/ppermute | solution.py:834
  437.1 22.9 %collective-permute-start.11 = (bf16[384,640]{1,0:T(8,128)(2,1)}, bf16[384,640]{1,0:T(8,128)(2,1)S(1)}, u32[]{:S(2)}, u32[]{:S(2)}) collective-permute-start(bf16[384,640]{1,0:T(8,128)(2,1)} %get-tuple-element.132), channel_id=1, source_target_pairs={{0,4},{1,5},{2,6},{3,7},{4,0},{5,1},{6,2},{7,3},{8,12},{9,13},{10,... | collective-permute-start | bytes 1474568 | tf_op jit(solution)/shard_map/ppermute | solution.py:834
  443.6 16.3 %collective-permute-start.12 = (bf16[384,640]{1,0:T(8,128)(2,1)}, bf16[384,640]{1,0:T(8,128)(2,1)S(1)}, u32[]{:S(2)}, u32[]{:S(2)}) collective-permute-start(bf16[384,640]{1,0:T(8,128)(2,1)} %get-tuple-element.133), channel_id=1, source_target_pairs={{0,6},{1,7},{2,4},{3,5},{4,2},{5,3},{6,0},{7,1},{8,14},{9,15},{10,... | collective-permute-start | bytes 1474568 | tf_op jit(solution)/shard_map/ppermute | solution.py:834
  460.2 10.6 %collective-permute-start.16 = (bf16[96,640]{1,0:T(8,128)(2,1)S(1)}, bf16[96,640]{1,0:T(8,128)(2,1)S(1)}, u32[]{:S(2)}, u32[]{:S(2)}) collective-permute-start(bf16[96,640]{1,0:T(8,128)(2,1)S(1)} %get-tuple-element.188), channel_id=1, source_target_pairs={{0,8},{8,0},{16,24},{24,16},{1,9},{9,1},{17,25},{25,17},{2,10},{10... | collective-permute-start | bytes 368648 | tf_op jit(solution)/shard_map/ppermute | solution.py:834
  460.3 10.9 %collective-permute-start.17 = (bf16[96,640]{1,0:T(8,128)(2,1)S(1)}, bf16[96,640]{1,0:T(8,128)(2,1)S(1)}, u32[]{:S(2)}, u32[]{:S(2)}) collective-permute-start(bf16[96,640]{1,0:T(8,128)(2,1)S(1)} %get-tuple-element.190), channel_id=1, source_target_pairs={{0,16},{8,24},{16,0},{24,8},{1,17},{9,25},{17,1},{25,9},{2,18},{10... | collective-permute-start | bytes 368648 | tf_op jit(solution)/shard_map/ppermute | solution.py:834
  462.3 8.9 %collective-permute-start.18 = (bf16[96,640]{1,0:T(8,128)(2,1)S(1)}, bf16[96,640]{1,0:T(8,128)(2,1)S(1)}, u32[]{:S(2)}, u32[]{:S(2)}) collective-permute-start(bf16[96,640]{1,0:T(8,128)(2,1)S(1)} %get-tuple-element.189), channel_id=1, source_target_pairs={{0,24},{8,16},{16,8},{24,0},{1,25},{9,17},{17,9},{25,1},{2,26},{10... | collective-permute-start | bytes 368648 | tf_op jit(solution)/shard_map/ppermute | solution.py:834
  465.4 22.0 %copy-start.1 = (f32[64,5096]{1,0:T(8,128)S(1)}, f32[64,5096]{1,0:T(8,128)}, u32[]{:S(2)}) copy-start(f32[64,5096]{1,0:T(8,128)} %param.29) | copy-start | bytes 3913732
  475.1 10.9 %all-to-all-start = ((f32[32,1,128]{2,1,0:T(1,128)}), f32[32,1,128]{2,1,0:T(1,128)S(1)}, u32[]{:S(2)}, u32[]{:S(2)}) async-start(f32[32,1,128]{2,1,0:T(1,128)} %broadcast_in_dim.21), calls=%async_computation | async-start | bytes 32768 | tf_op jit(solution)/shard_map/all_to_all | solution.py:883
  479.6 14.6 %collective-permute-start.19 = (bf16[96,640]{1,0:T(8,128)(2,1)}, bf16[96,640]{1,0:T(8,128)(2,1)}, u32[]{:S(2)}, u32[]{:S(2)}) collective-permute-start(bf16[96,640]{1,0:T(8,128)(2,1)} %get-tuple-element.181), channel_id=1, source_target_pairs={{0,8},{8,0},{16,24},{24,16},{1,9},{9,1},{17,25},{25,17},{2,10},{10... | collective-permute-start | bytes 368648 | tf_op jit(solution)/shard_map/ppermute | solution.py:834
  481.5 12.8 %collective-permute-start.20 = (bf16[96,640]{1,0:T(8,128)(2,1)}, bf16[96,640]{1,0:T(8,128)(2,1)}, u32[]{:S(2)}, u32[]{:S(2)}) collective-permute-start(bf16[96,640]{1,0:T(8,128)(2,1)} %get-tuple-element.181), channel_id=1, source_target_pairs={{0,16},{8,24},{16,0},{24,8},{1,17},{9,25},{17,1},{25,9},{2,18},{10... | collective-permute-start | bytes 368648 | tf_op jit(solution)/shard_map/ppermute | solution.py:834
  483.9 10.3 %collective-permute-start.21 = (bf16[96,640]{1,0:T(8,128)(2,1)}, bf16[96,640]{1,0:T(8,128)(2,1)}, u32[]{:S(2)}, u32[]{:S(2)}) collective-permute-start(bf16[96,640]{1,0:T(8,128)(2,1)} %get-tuple-element.181), channel_id=1, source_target_pairs={{0,24},{8,16},{16,8},{24,0},{1,25},{9,17},{17,9},{25,1},{2,26},{10... | collective-permute-start | bytes 368648 | tf_op jit(solution)/shard_map/ppermute | solution.py:834
  487.4 4.9 copy-start.4
  487.4 4.9 copy-start.8
  487.4 4.9 copy-start.9
  492.3 1.9 copy-start.12
  496.6 2.6 copy-start.22
  496.6 3.9 copy-start.19
  496.6 5.3 %copy-start.24 = (f32[8,40]{1,0:T(8,128)S(1)}, f32[8,40]{1,0:T(8,128)}, u32[]{:S(2)}) copy-start(f32[8,40]{1,0:T(8,128)} %param.32) | copy-start | bytes 3844
  496.6 6.6 %copy-start.5 = (f32[416,320]{1,0:T(8,128)S(1)}, f32[416,320]{1,0:T(8,128)}, u32[]{:S(2)}) copy-start(f32[416,320]{1,0:T(8,128)} %param.28) | copy-start | bytes 1597444
  496.6 6.6 %copy-start.10 = (f32[416,320]{1,0:T(8,128)S(1)}, f32[416,320]{1,0:T(8,128)}, u32[]{:S(2)}) copy-start(f32[416,320]{1,0:T(8,128)} %param.35) | copy-start | bytes 1597444
  496.7 6.6 %copy-start.11 = (f32[416,320]{1,0:T(8,128)S(1)}, f32[416,320]{1,0:T(8,128)}, u32[]{:S(2)}) copy-start(f32[416,320]{1,0:T(8,128)} %param.42) | copy-start | bytes 1597444
  503.3 1.6 copy-start.6
  503.3 1.6 copy-start.13
  503.3 1.6 copy-start.14
  503.3 1.6 copy-start.15
  503.3 1.6 copy-start.16
  503.3 1.7 copy-start.17
Sparse Core Ops, SparseCore 0:
  10.7 37.6 all-gather.10
  50.8 33.4 all-gather.8
  86.7 41.1 all-gather.6
